TPU v7x, 128 devices: a whole 4x4x4 slice. The times are simulated.
128 devices in a mesh: dp: 16 (over z, x), mp: 8 (over y, core).
Axes of the slice: x: 4, y: 4, z: 4, core: 2. Of those that a mesh axis runs over, the one named last changes fastest.
Arguments:
- gradient: bfloat16 [16, 768, 8, 768], P(None, 'dp', None, 'mp'), may hold values from -1.5 to 1.5
- owner: int32 [128], replicated, may hold values from 0 to 127, as said below
- left_stat: float32 [16, 8, 2, 768, 768], P('dp', 'mp'), may hold values from -2 to 10, as said below
- right_stat: float32 [16, 8, 2, 768, 768], P('dp', 'mp'), may hold values from -2 to 10, as said below
- left_root: bfloat16 [16, 8, 2, 768, 768], P('dp', 'mp'), may hold values from -1 to 2, as said below
- right_root: bfloat16 [16, 8, 2, 768, 768], P('dp', 'mp'), may hold values from -1 to 2, as said below
Outputs:
- precond: bfloat16 [16, 768, 8, 768], P(None, 'dp', None, 'mp')
- left_new: float32 [16, 8, 2, 768, 768], P('dp', 'mp')
- right_new: float32 [16, 8, 2, 768, 768], P('dp', 'mp')
Inputs may be any that keep to these rules, and one draw needn't show every extreme that they name: No owner is named by more than 2 blocks, and one owner is named by exactly 2. `left_stat`: Symmetric. `right_stat`: Symmetric. `left_root`: Symmetric. `right_root`: Symmetric.
All inputs are finite; a program needn't handle non-finite values.
Results may differ from a plain program's by a relative error of at most 0.0049.
Values may be sent and summed in bfloat16 or wider, within the bound.
No kernel may reach another device: no remote copies, remote signals or barrier semaphores. Data moves between devices by JAX's collectives and lax.ppermute only.
A program may use at most 128 MiB of HBM per device.

v0:
```python
import jax
import jax.numpy as jnp
from jax import lax
from jax.sharding import PartitionSpec as P

stat_decay = 0.98


def routing(owner, slots, devices, row_blocks, col_blocks):
    count = owner.shape[0]
    positions = jnp.arange(count, dtype=jnp.int32)
    earlier = (owner[None, :] == owner[:, None]) & (positions[None, :] < positions[:, None])
    rank = jnp.sum(earlier.astype(jnp.int32), axis=1)
    target = owner * slots + rank
    columns = jnp.arange(devices * slots, dtype=jnp.int32)
    table = (target[:, None] == columns[None, :]).astype(jnp.bfloat16)
    return table.reshape(row_blocks, col_blocks, devices * slots)


def per_device(gradient, owner, left_stat, right_stat, left_root, right_root):
    row_blocks, row_part, col_blocks, col_part = gradient.shape
    dp_count = lax.axis_size("dp")
    mp_count = lax.axis_size("mp")
    devices = dp_count * mp_count
    slots = left_stat.shape[2]
    width = left_stat.shape[3]
    table = routing(owner, slots, devices, row_blocks, col_blocks)
    outgoing = jnp.einsum(
        "rcd,rpcq->dpq", table, gradient, preferred_element_type=jnp.float32
    ).astype(jnp.bfloat16)
    arrived = lax.all_to_all(
        outgoing.reshape(devices, slots, row_part, col_part),
        ("dp", "mp"),
        split_axis=0,
        concat_axis=0,
        tiled=True,
    )
    arrived = arrived.reshape(dp_count, mp_count, slots, row_part, col_part)
    left_gram = jnp.einsum(
        "amspq,bmsuq->sapbu", arrived, arrived, preferred_element_type=jnp.float32
    ).reshape(slots, width, width)
    right_gram = jnp.einsum(
        "amspq,anspv->smqnv", arrived, arrived, preferred_element_type=jnp.float32
    ).reshape(slots, width, width)
    left_new = stat_decay * left_stat[0, 0] + (1.0 - stat_decay) * left_gram
    right_new = stat_decay * right_stat[0, 0] + (1.0 - stat_decay) * right_gram
    left_view = left_root[0, 0].reshape(slots, dp_count, row_part, dp_count, row_part)
    right_view = right_root[0, 0].reshape(slots, mp_count, col_part, mp_count, col_part)
    half = jnp.einsum(
        "sapbu,bmsuq->amspq", left_view, arrived, preferred_element_type=jnp.float32
    ).astype(jnp.bfloat16)
    leaving = jnp.einsum(
        "amspq,smqnv->anspv", half, right_view, preferred_element_type=jnp.float32
    ).astype(jnp.bfloat16)
    returned = lax.all_to_all(
        leaving.reshape(devices, slots, row_part, col_part),
        ("dp", "mp"),
        split_axis=0,
        concat_axis=0,
        tiled=True,
    )
    returned = returned.reshape(devices * slots, row_part, col_part)
    precond = jnp.einsum(
        "rcd,dpq->rpcq", table, returned, preferred_element_type=jnp.float32
    ).astype(jnp.bfloat16)
    return (precond, left_new[None, None], right_new[None, None])


def solution(mesh):
    return jax.shard_map(
        per_device,
        mesh=mesh,
        in_specs=(
            P(None, "dp", None, "mp"),
            P(),
            P("dp", "mp", None, None, None),
            P("dp", "mp", None, None, None),
            P("dp", "mp", None, None, None),
            P("dp", "mp", None, None, None),
        ),
        out_specs=(
            P(None, "dp", None, "mp"),
            P("dp", "mp", None, None, None),
            P("dp", "mp", None, None, None),
        ),
        check_vma=False,
    )
```

profile of v0, /device:TPU:1, one launch (start us, length us, event | category | flops | bytes accessed | tf_op | source)
XLA Modules:
  0.0 156.6 jit_solution(18153787720875951097)
XLA Ops:
  0.6 0.0 copy-start
  0.6 1.0 convert_reduce_fusion
  1.6 0.7 multiply_add_fusion.2
  2.3 0.1 eq.53
  2.4 0.1 copy.44
  2.4 0.0 copy-done
  2.4 2.7 %bitcast_convert_fusion.2 = bf16[256,48,96]{0,2,1:T(8,128)(2,1)} fusion(bf16[16,48,8,96]{3,2,1,0:T(8,128)(2,1)S(1)} %copy-done, s32[16,8]{0,1:T(8,128)S(1)} %copy.44), kind=kOutput, calls=%fused_computation.6 | convolution fusion | flops 303202304 | bytes 3539456 | tf_op jit(solution)/shard_map/rcd,rpcq->dpq/dot_general | solution.py:28
  5.1 4.7 %copy.46 = bf16[256,48,96]{2,1,0:T(8,128)(2,1)} copy(bf16[256,48,96]{0,2,1:T(8,128)(2,1)} %bitcast_convert_fusion.2) | data formatting | bytes 4718592 | tf_op jit(solution)/shard_map/convert_element_type | solution.py:30
  9.8 11.9 %all-to-all-start = ((bf16[128,2,48,96]{3,2,1,0:T(8,128)(2,1)}), bf16[128,2,48,96]{3,2,1,0:T(8,128)(2,1)}, u32[]{:S(2)}, u32[]{:S(2)}) async-start(bf16[128,2,48,96]{3,2,1,0:T(8,128)(2,1)} %bitcast.62), calls=%async_computation | async-start | bytes 6291456 | tf_op jit(solution)/shard_map/all_to_all | solution.py:31
  21.7 10.0 %reshape_squeeze.6 = bf16[2,16,48,16,48]{4,3,2,1,0:T(8,128)(2,1)} reshape(bf16[1,1,2,768,768]{4,3,2,1,0:T(8,128)(2,1)} %param.10) | data formatting | bytes 4718592 | tf_op jit(solution)/shard_map/reshape;squeeze | solution.py:47
  31.7 6.4 %reshape_squeeze.7 = bf16[2,8,96,8,96]{4,3,2,1,0:T(8,128)(2,1)} reshape(bf16[1,1,2,768,768]{4,3,2,1,0:T(8,128)(2,1)} %param.11) | data formatting | bytes 4718592 | tf_op jit(solution)/shard_map/reshape;squeeze | solution.py:48
  38.1 25.2 %all-to-all-done = bf16[128,2,48,96]{3,2,1,0:T(8,128)(2,1)} async-done(((bf16[128,2,48,96]{3,2,1,0:T(8,128)(2,1)}), bf16[128,2,48,96]{3,2,1,0:T(8,128)(2,1)}, u32[]{:S(2)}, u32[]{:S(2)}) %all-to-all-start) | async-done | bytes 2359328 | tf_op jit(solution)/shard_map/all_to_all | solution.py:31
  63.3 11.0 %bitcast_convert_fusion = bf16[2,16,48,8,96]{4,2,3,1,0:T(8,128)(2,1)} fusion(bf16[2,8,96,8,96,1]{4,3,2,1,0,5:T(8,128)(2,1)} %bitcast.65, bf16[2,16,48,16,48,1]{4,3,2,1,0,5:T(8,128)(2,1)} %bitcast.63, bf16[16,8,2,48,96,1]{4,3,2,1,0,5:T(8,128)(2,1)} %bitcast.5), kind=kOutput, calls=%fused_computation.2 | convolution fusion | flops 3626237952 | bytes 9437184 | tf_op jit(solution)/shard_map/amspq,smqnv->anspv/dot_general | solution.py:52
  74.3 4.1 %copy.50 = bf16[128,2,48,96]{3,2,1,0:T(8,128)(2,1)} copy(bf16[128,2,48,96]{3,2,0,1:T(8,128)(2,1)} %bitcast.64) | data formatting | bytes 4718592 | tf_op jit(solution)/shard_map/reshape | solution.py:56
  78.4 5.3 %all-to-all-start.1 = ((bf16[128,2,48,96]{3,2,1,0:T(8,128)(2,1)}), bf16[128,2,48,96]{3,2,1,0:T(8,128)(2,1)}, u32[]{:S(2)}, u32[]{:S(2)}) async-start(bf16[128,2,48,96]{3,2,1,0:T(8,128)(2,1)} %copy.50), calls=%async_computation.1 | async-start | bytes 6291456 | tf_op jit(solution)/shard_map/all_to_all | solution.py:55
  83.7 11.5 %bitcast_multiply_fusion = f32[2,16,48,16,48]{4,2,3,1,0:T(8,128)} fusion(bf16[16,8,2,48,96,1]{4,3,2,1,0,5:T(8,128)(2,1)} %bitcast.5), kind=kOutput, calls=%fused_computation | convolution fusion | flops 1813118976 | bytes 7077888 | tf_op jit(solution)/shard_map/amspq,bmsuq->sapbu/dot_general | solution.py:39
  95.2 14.2 %copy.55 = f32[2,16,48,16,48]{4,3,2,1,0:T(8,128)} copy(f32[2,16,48,16,48]{4,2,3,1,0:T(8,128)} %bitcast_multiply_fusion) | data formatting | bytes 9437184 | tf_op jit(solution)/shard_map/mul | solution.py:45
  109.4 10.9 %mul.44 = f32[1,1,2,768,768]{4,3,2,1,0:T(8,128)} reshape(f32[2,16,48,16,48]{4,3,2,1,0:T(8,128)} %copy.55) | data formatting | bytes 9437184 | tf_op jit(solution)/shard_map/mul | solution.py:45
  120.3 5.7 %bitcast_multiply_fusion.1 = f32[2,8,96,8,96]{4,2,3,1,0:T(8,128)S(1)} fusion(bf16[16,8,2,48,96,1]{4,3,2,1,0,5:T(8,128)(2,1)} %bitcast.5), kind=kOutput, calls=%fused_computation.1 | convolution fusion | flops 1813118976 | bytes 7077888 | tf_op jit(solution)/shard_map/amspq,anspv->smqnv/dot_general | solution.py:42
  126.0 7.5 %copy.58 = f32[2,8,96,8,96]{4,3,2,1,0:T(8,128)} copy(f32[2,8,96,8,96]{4,2,3,1,0:T(8,128)S(1)} %bitcast_multiply_fusion.1) | data formatting | bytes 9437184 | tf_op jit(solution)/shard_map/mul | solution.py:46
  133.5 7.4 %mul.47 = f32[1,1,2,768,768]{4,3,2,1,0:T(8,128)} reshape(f32[2,8,96,8,96]{4,3,2,1,0:T(8,128)} %copy.58) | data formatting | bytes 9437184 | tf_op jit(solution)/shard_map/mul | solution.py:46
  140.9 11.4 %multiply_add_fusion = (f32[1,1,2,768,768]{4,3,2,1,0:T(8,128)}, f32[1,1,2,768,768]{4,3,2,1,0:T(8,128)}) fusion(f32[1,1,2,768,768]{4,3,2,1,0:T(8,128)} %mul.47, f32[1,1,2,768,768]{4,3,2,1,0:T(8,128)} %param.9, f32[1,1,2,768,768]{4,3,2,1,0:T(8,128)} %mul.44, f32[1,1,2,768,768]{4,3,2,1,0:T(8,128)} %param.8), kind=kLoop, calls=%fused_computation.7 | loop fusion | flops 4718592 | bytes 28311552 | tf_op jit(solution)/shard_map/add | solution.py:46
  152.3 0.0 all-to-all-done.1
  152.3 0.0 copy-start.1
  152.3 2.8 %fusion.38 = bf16[16,48,8,96]{3,0,2,1:T(8,128)(2,1)S(1)} fusion(bf16[256,48,96,1]{2,1,0,3:T(8,128)(2,1)} %bitcast.18, s32[16,8]{0,1:T(8,128)S(1)} %copy.44), kind=kOutput, calls=%fused_computation.22 | convolution fusion | flops 302612480 | bytes 3539456 | tf_op jit(solution)/shard_map/rcd,dpq->rpcq/dot_general | solution.py:63
  155.0 1.6 copy.59
  156.6 0.0 copy-done.1
Async XLA Ops:
  0.6 1.8 %copy-start = (bf16[16,48,8,96]{3,2,1,0:T(8,128)(2,1)S(1)}, bf16[16,48,8,96]{3,2,1,0:T(8,128)(2,1)}, u32[]{:S(2)}) copy-start(bf16[16,48,8,96]{3,2,1,0:T(8,128)(2,1)} %param.6) | copy-start | bytes 3538948
  9.8 53.5 %all-to-all-start = ((bf16[128,2,48,96]{3,2,1,0:T(8,128)(2,1)}), bf16[128,2,48,96]{3,2,1,0:T(8,128)(2,1)}, u32[]{:S(2)}, u32[]{:S(2)}) async-start(bf16[128,2,48,96]{3,2,1,0:T(8,128)(2,1)} %bitcast.62), calls=%async_computation | async-start | bytes 6291456 | tf_op jit(solution)/shard_map/all_to_all | solution.py:31
  78.4 73.9 %all-to-all-start.1 = ((bf16[128,2,48,96]{3,2,1,0:T(8,128)(2,1)}), bf16[128,2,48,96]{3,2,1,0:T(8,128)(2,1)}, u32[]{:S(2)}, u32[]{:S(2)}) async-start(bf16[128,2,48,96]{3,2,1,0:T(8,128)(2,1)} %copy.50), calls=%async_computation.1 | async-start | bytes 6291456 | tf_op jit(solution)/shard_map/all_to_all | solution.py:55
  152.3 4.3 %copy-start.1 = (bf16[16,48,8,96]{3,2,1,0:T(8,128)(2,1)S(1)}, bf16[16,48,8,96]{3,2,1,0:T(8,128)(2,1)}, u32[]{:S(2)}) copy-start(bf16[16,48,8,96]{3,2,1,0:T(8,128)(2,1)} %param.6) | copy-start | bytes 3538948
where the time goes:
time: 158 us; the launch traced here: 157 us
  local copies, waits for them, and re-layouts  66.8 us (42%)
  matrix products  33.6 us (21%)
  waiting for transfers between devices  25.2 us (16%)
  starting transfers between devices  17.2 us (11%)
  other arithmetic  13 us (8%)
    all_to_all x1, waiting for transfers between devices, per_device(): lax.all_to_all(outgoing.reshape(devices, slots, row_part, col_part), ('dp...  25.2 us
    mul x2, local copies, waits for them, and re-layouts, per_device(): left_new = stat_decay * left_stat[0, 0] + (1.0 - stat_decay) * left_gram  25.1 us
    mul x2, local copies, waits for them, and re-layouts, per_device(): right_new = stat_decay * right_stat[0, 0] + (1.0 - stat_decay) * right_gram  14.9 us
    all_to_all x1, starting transfers between devices, per_device(): lax.all_to_all(outgoing.reshape(devices, slots, row_part, col_part), ('dp...  11.9 us
    dot_general x1, matrix products, per_device(): jnp.einsum('amspq,bmsuq->sapbu', arrived, arrived, preferred_element_type...  11.5 us
    add x1, other arithmetic, per_device(): right_new = stat_decay * right_stat[0, 0] + (1.0 - stat_decay) * right_gram  11.4 us
    dot_general x1, matrix products, per_device(): jnp.einsum('amspq,smqnv->anspv', half, right_view, preferred_element_type...  11 us
    another operation x1, local copies, waits for them, and re-layouts, per_device(): left_root[0, 0].reshape(slots, dp_count, row_part, dp_count, row_part)  9.98 us
  transfers between devices with their start and end apart: 2, of which 1 were waited for; matrix products, arithmetic and copies ran while one was open for 54% of the time, Pallas kernels for 0%

commit v1 on v0

v1 whole, which is shorter than its diff:
```python
import jax
import jax.numpy as jnp
from jax import lax
from jax.experimental import pallas as pl
from jax.experimental.pallas import tpu as pltpu
from jax.sharding import PartitionSpec as P

STAT_DECAY = 0.98
LANES = 128
F32 = jnp.float32
BF16 = jnp.bfloat16
MIB = 1024 * 1024
FALLBACK = True
HBM = pltpu.HBM
FIRST_SPANS = (8, 4, 4)
SPANS = (8, 8)


def spread_matrix(part, groups):
    row = lax.broadcasted_iota(jnp.int32, (groups * LANES, groups * part), 0)
    col = lax.broadcasted_iota(jnp.int32, (groups * LANES, groups * part), 1)
    hit = (row // LANES == col // part) & (row % LANES == col % part)
    return jnp.where(hit, 1.0, 0.0).astype(BF16)


def count_slots(owner_ref, seen_ref, block):
    dest = owner_ref[block]
    slot = seen_ref[dest]
    seen_ref[dest] = slot + 1
    return dest, slot


def clear_counts(seen_ref, devices):
    def clear(i, carry):
        seen_ref[i] = 0
        return carry

    lax.fori_loop(0, devices, clear, 0)


def pack_kernel(owner_ref, grad_ref, out_ref, rows_ref, seen_ref):
    row_blocks, row_part, col_blocks, col_part = grad_ref.shape
    devices, slots = out_ref.shape[:2]
    clear_counts(seen_ref, devices)
    rows_ref[...] = jnp.zeros_like(rows_ref)

    def clear(i, carry):
        for s in range(slots):
            out_ref[i, s] = jnp.zeros((row_part, LANES), BF16)
        return carry

    lax.fori_loop(0, devices, clear, 0)

    def block_row(r, carry):
        rows_ref[:, :col_part] = grad_ref[r].astype(F32).reshape(row_part * col_blocks, col_part)
        for c in range(col_blocks):
            dest, slot = count_slots(owner_ref, seen_ref, r * col_blocks + c)
            tile = rows_ref[pl.ds(c, row_part, stride=col_blocks), :]
            out_ref[dest, slot] = tile.astype(BF16)
        return carry

    lax.fori_loop(0, row_blocks, block_row, 0)


def unpack_kernel(owner_ref, back_ref, out_ref, rows_ref, seen_ref):
    row_blocks, row_part, col_blocks, col_part = out_ref.shape
    devices = back_ref.shape[0]
    clear_counts(seen_ref, devices)

    def block_row(r, carry):
        for c in range(col_blocks):
            dest, slot = count_slots(owner_ref, seen_ref, r * col_blocks + c)
            rows_ref[pl.ds(c, row_part, stride=col_blocks), :] = back_ref[dest, slot].astype(F32)
        rows = rows_ref[:, :col_part].reshape(row_part, col_blocks, col_part)
        out_ref[r] = rows.astype(BF16)
        return carry

    lax.fori_loop(0, row_blocks, block_row, 0)


def pad_kernel(root_ref, out_ref):
    width = root_ref.shape[1]
    part = width // (out_ref.shape[1] // LANES)
    groups = LANES // (LANES - part)
    spread = spread_matrix(part, groups)
    wide, narrow = spread.shape
    for g in range(width // narrow):
        rows = jnp.dot(spread, root_ref[0, g * narrow : (g + 1) * narrow, :], preferred_element_type=F32).astype(BF16)
        for h in range(width // narrow):
            cell = lax.dot_general(
                rows[:, h * narrow : (h + 1) * narrow], spread, (((1,), (1,)), ((), ())), preferred_element_type=F32
            )
            out_ref[0, g * wide : (g + 1) * wide, h * wide : (h + 1) * wide] = cell.astype(BF16)


def gather_tiles(arr_ref, wide_ref):
    row_groups, col_groups, _, row_part, _ = arr_ref.shape
    for a in range(row_groups):
        for m in range(col_groups):
            wide_ref[a * row_part : (a + 1) * row_part, m * LANES : (m + 1) * LANES] = arr_ref[a, m, 0]


def precond_kernel(arr_ref, left_ref, right_ref, out_ref, wide_ref):
    row_groups, col_groups, _, row_part, _ = arr_ref.shape
    gather_tiles(arr_ref, wide_ref)
    step = 4 * row_part
    for i in range(row_groups // 4):
        half = jnp.dot(left_ref[0, i * step : (i + 1) * step, :], wide_ref[...], preferred_element_type=F32).astype(BF16)
        result = jnp.dot(half, right_ref[0], preferred_element_type=F32).astype(BF16)
        for k in range(4):
            for m in range(col_groups):
                out_ref[4 * i + k, m, 0] = result[k * row_part : (k + 1) * row_part, m * LANES : (m + 1) * LANES]


def gram_kernel(arr_ref, left_ref, right_ref, left_out, right_out, wide_ref, block_ref):
    width = block_ref.shape[0]
    part = width // arr_ref.shape[1]
    tile = left_ref.shape[1]
    step = pl.program_id(1)

    @pl.when(step == 0)
    def _():
        gather_tiles(arr_ref, wide_ref)
        spread = spread_matrix(part, LANES // (LANES - part))
        wide, narrow = spread.shape
        for g in range(width // narrow):
            cols = jnp.dot(wide_ref[:, g * wide : (g + 1) * wide], spread, preferred_element_type=F32)
            block_ref[:, g * narrow : (g + 1) * narrow] = cols.astype(BF16)

    for i in range(width // tile):

        @pl.when(step == i)
        def _(i=i):
            mine = slice(i * tile, (i + 1) * tile)
            left = lax.dot_general(
                block_ref[mine, :], block_ref[...], (((1,), (1,)), ((), ())), preferred_element_type=F32
            )
            left_out[0] = STAT_DECAY * left_ref[0] + (1.0 - STAT_DECAY) * left
            right = lax.dot_general(
                block_ref[:, mine], block_ref[...], (((0,), (0,)), ((), ())), preferred_element_type=F32
            )
            right_out[0] = STAT_DECAY * right_ref[0] + (1.0 - STAT_DECAY) * right


def general_path(gradient, owner, left_stat, right_stat, left_root, right_root):
    row_blocks, row_part, col_blocks, col_part = gradient.shape
    dp_count = lax.axis_size("dp")
    mp_count = lax.axis_size("mp")
    devices = dp_count * mp_count
    slots, width = left_stat.shape[2:4]
    wide = mp_count * LANES
    smem = pl.BlockSpec(memory_space=pltpu.SMEM)
    vmem = pl.BlockSpec(memory_space=pltpu.VMEM)
    rows_scratch = pltpu.VMEM((row_part * col_blocks, LANES), F32)
    seen_scratch = pltpu.SMEM((devices,), jnp.int32)

    def exchange(x):
        return lax.all_to_all(x, ("dp", "mp"), split_axis=0, concat_axis=0, tiled=True)

    outgoing = pl.pallas_call(
        pack_kernel,
        out_shape=jax.ShapeDtypeStruct((devices, slots, row_part, LANES), BF16),
        in_specs=[smem, vmem],
        out_specs=vmem,
        scratch_shapes=[rows_scratch, seen_scratch],
        compiler_params=pltpu.CompilerParams(vmem_limit_bytes=12 * MIB),
        name="pack",
    )(owner, gradient)
    padded_root = pl.pallas_call(
        pad_kernel,
        grid=(slots,),
        out_shape=jax.ShapeDtypeStruct((slots, wide, wide), BF16),
        in_specs=[pl.BlockSpec((1, width, width), lambda s: (s, 0, 0))],
        out_specs=pl.BlockSpec((1, wide, wide), lambda s: (s, 0, 0)),
        cost_estimate=pl.CostEstimate(flops=slots * 4 * 10**9, bytes_accessed=7 * 10**6, transcendentals=0),
        compiler_params=pltpu.CompilerParams(vmem_limit_bytes=24 * MIB),
        name="pad_right_root",
    )(right_root[0, 0])
    tiles = (dp_count, mp_count, slots, row_part, LANES)
    arrived = exchange(outgoing).reshape(tiles)
    tile_spec = pl.BlockSpec((dp_count, mp_count, 1, row_part, LANES), lambda s, *_: (0, 0, s, 0, 0))
    leaving = pl.pallas_call(
        precond_kernel,
        grid=(slots,),
        out_shape=jax.ShapeDtypeStruct(tiles, BF16),
        in_specs=[
            tile_spec,
            pl.BlockSpec((1, width, width), lambda s: (s, 0, 0)),
            pl.BlockSpec((1, wide, wide), lambda s: (s, 0, 0)),
        ],
        out_specs=tile_spec,
        scratch_shapes=[pltpu.VMEM((width, wide), BF16)],
        cost_estimate=pl.CostEstimate(flops=slots * 3 * 10**9, bytes_accessed=13 * 10**6, transcendentals=0),
        compiler_params=pltpu.CompilerParams(vmem_limit_bytes=30 * MIB),
        name="precondition",
    )(arrived, left_root[0, 0], padded_root)
    returned = exchange(leaving.reshape(outgoing.shape))
    tile = width // 3
    stat_spec = pl.BlockSpec((1, tile, width), lambda s, i: (s, i, 0))
    left_new, right_new = pl.pallas_call(
        gram_kernel,
        grid=(slots, width // tile),
        out_shape=[jax.ShapeDtypeStruct((slots, width, width), F32)] * 2,
        in_specs=[tile_spec, stat_spec, stat_spec],
        out_specs=[stat_spec, stat_spec],
        scratch_shapes=[pltpu.VMEM((width, wide), BF16), pltpu.VMEM((width, width), BF16)],
        cost_estimate=pl.CostEstimate(flops=slots * 3 * 10**9, bytes_accessed=22 * 10**6, transcendentals=0),
        compiler_params=pltpu.CompilerParams(vmem_limit_bytes=30 * MIB),
        name="grams",
    )(arrived, left_stat[0, 0], right_stat[0, 0])
    precond = pl.pallas_call(
        unpack_kernel,
        out_shape=jax.ShapeDtypeStruct(gradient.shape, BF16),
        in_specs=[smem, vmem],
        out_specs=vmem,
        scratch_shapes=[rows_scratch, seen_scratch],
        compiler_params=pltpu.CompilerParams(vmem_limit_bytes=12 * MIB),
        name="unpack",
    )(owner, returned)
    return (precond, left_new[None, None], right_new[None, None])


def copy_in(src, dst, sem):
    copy = pltpu.make_async_copy(src, dst, sem)
    copy.start()
    return copy


def lane_of(shape):
    return lax.broadcasted_iota(jnp.int32, shape, len(shape) - 1)


def pack_pairs_kernel(
    owner_hbm, grad_hbm, out_hbm, table_hbm, bad_hbm, owner_ref, grad_ref, out_ref, rows_ref, table_ref, bad_ref, seen_ref, first_ref,
    pairs_ref, load_sems, store_sems, sems,
):
    row_blocks, row_part, col_blocks, col_part = grad_ref.shape
    devices, height = out_hbm.shape[:2]
    count = row_blocks * col_blocks
    tall = row_part * col_blocks
    chunks = load_sems.shape[0]
    span = row_blocks // chunks
    owner_copy = copy_in(owner_hbm, owner_ref, sems.at[0])
    copies = []
    for i in range(chunks):
        part = pl.ds(i * span, span)
        copies.append(copy_in(grad_hbm.at[part], grad_ref.at[part], load_sems.at[i]))
    me = lax.axis_index("dp") * lax.axis_size("mp") + lax.axis_index("mp")
    half = col_part // 2
    free = LANES - col_part
    rest = half - free
    groups = row_part // 8
    extras_at = devices
    info_at = 2 * devices

    def clear(i, carry):
        seen_ref[i] = 0
        pairs_ref[i] = 0
        first_ref[i] = count
        return carry

    lax.fori_loop(0, devices, clear, 0, unroll=8)
    rows_ref[pl.ds(row_blocks * tall, tall), :] = jnp.zeros((tall, LANES), F32)
    owner_copy.wait()

    def block_row(r, extras):
        rows_ref[pl.ds(r * tall, tall), col_part:] = jnp.zeros((tall, free), F32)
        rows_ref[pl.ds(r * tall, tall), :col_part] = grad_ref[r].astype(F32).reshape(tall, col_part)
        for c in range(col_blocks):
            block = r * col_blocks + c
            dest, slot = count_slots(owner_ref, seen_ref, block)
            table_ref[block] = jnp.where(slot == 0, dest, 0)
            first_ref[jnp.where(slot == 0, dest, devices)] = block
            table_ref[extras_at + extras] = block
            extras = extras + slot
        return extras

    extras = jnp.int32(0)
    for i in range(chunks):
        copies[i].wait()
        extras = lax.fori_loop(i * span, (i + 1) * span, block_row, extras)
    for i in range(3):
        table_ref[info_at + i] = 0
    table_ref[info_at + 3] = extras
    bad_ref[0] = 0

    def note(e, carry):
        dest = owner_ref[table_ref[extras_at + e]]
        pairs = pairs_ref[dest // 2]
        pairs_ref[dest // 2] = pairs + 1
        here = dest // 2 == me // 2
        table_ref[info_at] = jnp.where(here, 1, table_ref[info_at])
        table_ref[info_at + 1] = jnp.where(here, dest % 2, table_ref[info_at + 1])
        table_ref[info_at + 2] = jnp.where(dest == me, 1, table_ref[info_at + 2])
        bad_ref[0] = jnp.where(pairs > 0, 1, bad_ref[0])
        return carry

    lax.fori_loop(0, extras, note, 0)
    table_copy = copy_in(table_ref, table_hbm, sems.at[1])
    bad_copy = copy_in(bad_ref, bad_hbm, sems.at[2])

    def tile_of(block):
        return rows_ref[pl.ds(block // col_blocks * tall + block % col_blocks, row_part, stride=col_blocks), :]

    def message(d, carry):
        tile = tile_of(first_ref[d])
        out_ref[d] = jnp.concatenate([tile, jnp.zeros((height - row_part, LANES), F32)], axis=0).astype(BF16)
        return carry

    stores = []
    share = devices // chunks
    for i in range(chunks):
        lax.fori_loop(i * share, (i + 1) * share, message, 0, unroll=8)

        def extra(e, carry, i=i):
            block = table_ref[extras_at + e]
            chip = owner_ref[block] // 2

            @pl.when(2 * chip // share == i)
            def _():
                tile = tile_of(block)
                lane = lane_of((row_part, LANES))
                lane8 = lane_of((8, LANES))
                for j in range(2):
                    old = out_ref[2 * chip + j].astype(F32)
                    moved = pltpu.roll(tile, (col_part - half * j) % LANES, 1)
                    top = jnp.where(lane < col_part, old[:row_part], moved)
                    low = jnp.zeros((8, LANES), F32)
                    for k in range(groups):
                        piece = pltpu.roll(tile[8 * k : 8 * k + 8], (rest * k - half * j - free) % LANES, 1)
                        low = jnp.where(lane8 // rest == k, piece, low)
                    out_ref[2 * chip + j] = jnp.concatenate([top, low], axis=0).astype(BF16)

            return carry

        lax.fori_loop(0, extras, extra, 0)
        part = pl.ds(i * share, share)
        stores.append(copy_in(out_ref.at[part], out_hbm.at[part], store_sems.at[i]))
    table_copy.wait()
    bad_copy.wait()
    for store in stores:
        store.wait()


def unpack_pairs_kernel(owner_hbm, table_hbm, back_ref, out_hbm, owner_ref, table_ref, out_ref, rows_ref, sems, store_sems):
    row_blocks, row_part, col_blocks, col_part = out_ref.shape
    devices = back_ref.shape[0]
    owner_copy = copy_in(owner_hbm, owner_ref, sems.at[0])
    table_copy = copy_in(table_hbm, table_ref, sems.at[1])
    half = col_part // 2
    free = LANES - col_part
    rest = half - free
    groups = row_part // 8
    chunks = store_sems.shape[0]
    span = row_blocks // chunks
    owner_copy.wait()
    table_copy.wait()

    def finish(r, buffer):
        rows = rows_ref[buffer, :, :col_part].reshape(row_part, col_blocks, col_part)
        out_ref[r] = rows.astype(BF16)

    def block_row(r, buffer):
        for c in range(col_blocks):
            tile = back_ref[table_ref[r * col_blocks + c], :row_part, :]
            rows_ref[buffer, pl.ds(c, row_part, stride=col_blocks), :] = tile.astype(F32)
        finish(r, buffer)

    def body(t, carry):
        block_row(2 * t, 0)
        block_row(2 * t + 1, 1)
        return carry

    stores = []
    for i in range(chunks):
        lax.fori_loop(i * span // 2, (i + 1) * span // 2, body, 0)

        def extra(e, carry, i=i):
            block = table_ref[devices + e]
            chip = owner_ref[block] // 2
            r = block // col_blocks

            @pl.when(r // span == i)
            def _():
                lane = lane_of((row_part, LANES))
                tile = jnp.zeros((row_part, LANES), F32)
                for j in range(2):
                    message = back_ref[2 * chip + j].astype(F32)
                    top = pltpu.roll(message[:row_part], (half * j - col_part) % LANES, 1)
                    low = [
                        pltpu.roll(message[row_part : row_part + 8], (half * j + free - rest * k) % LANES, 1)
                        for k in range(groups)
                    ]
                    low = jnp.concatenate(low, axis=0)
                    tile = jnp.where((lane >= half * j) & (lane < half * j + free), top, tile)
                    tile = jnp.where((lane >= half * j + free) & (lane < half * j + half), low, tile)
                rows_ref[0, :, :col_part] = out_ref[r].astype(F32).reshape(row_part * col_blocks, col_part)
                rows_ref[0, pl.ds(block % col_blocks, row_part, stride=col_blocks), :] = tile
                finish(r, 0)

            return carry

        lax.fori_loop(0, table_ref[2 * devices + 3], extra, 0)
        part = pl.ds(i * span, span)
        stores.append(copy_in(out_ref.at[part], out_hbm.at[part], store_sems.at[i]))
    for store in stores:
        store.wait()


def halves_order(shape, core, axis, part, groups):
    half = part // 2
    free = LANES - part
    rest = half - free
    n = lax.broadcasted_iota(jnp.int32, shape, axis)
    tail = n - free * groups
    first = part * (n // free) + n % free
    second = part * (tail // rest) + free + tail % rest
    return half * core + jnp.where(tail < 0, first, second)


def swap_groups(rows, rest):
    rows = list(rows)
    count = len(rows)
    group = lane_of(rows[0].shape) // rest
    bit = 1
    while bit < count:
        low = group // bit % 2 == 0
        for i in range(count):
            if i // bit % 2 == 0:
                x, y = rows[i], rows[i + bit]
                rows[i] = jnp.where(low, x, pltpu.roll(y, rest * bit, 1))
                rows[i + bit] = jnp.where(low, pltpu.roll(x, LANES - rest * bit, 1), y)
        bit *= 2
    return rows


def prepare_kernel(
    table_ref, left_hbm, right_hbm, left_other_hbm, right_other_hbm, padded_ref, picked_ref, left0_ref, left1_ref, root_ref, root1_ref,
    sems,
):
    width = root_ref.shape[0]
    groups = padded_ref.shape[0] // LANES
    part = width // groups
    half = width // 2
    core = lax.axis_index("mp") % 2
    info_at = table_ref.shape[0] - LANES
    left0_copy = copy_in(left_hbm.at[0], left0_ref, sems.at[0])
    root_copy = copy_in(right_hbm.at[0], root_ref, sems.at[1])
    from_other = (table_ref[info_at] == 1) & (table_ref[info_at + 1] != core)

    @pl.when(from_other)
    def _():
        right = copy_in(right_other_hbm.at[1], root1_ref, sems.at[2])
        copy_in(left_other_hbm.at[1], left1_ref, sems.at[3]).wait()
        right.wait()

    @pl.when(jnp.logical_not(from_other))
    def _():
        right = copy_in(right_hbm.at[1], root1_ref, sems.at[2])
        copy_in(left_hbm.at[1], left1_ref, sems.at[3]).wait()
        right.wait()

    mine = jnp.where(
        halves_order((width, half), core, 1, part, groups) == lax.broadcasted_iota(jnp.int32, (width, half), 0), 1.0, 0.0
    ).astype(BF16)
    cols = jnp.dot(root1_ref[...], mine, preferred_element_type=F32).astype(BF16)
    for j in range(2):
        theirs = jnp.where(
            halves_order((half, width), j, 0, part, groups) == lax.broadcasted_iota(jnp.int32, (half, width), 1), 1.0, 0.0
        ).astype(BF16)
        picked_ref[j * half : (j + 1) * half, :] = jnp.dot(theirs, cols, preferred_element_type=F32).astype(BF16)
    root_copy.wait()
    spread = spread_matrix(part, LANES // (LANES - part))
    wide, narrow = spread.shape
    for g in range(width // narrow):
        rows = jnp.dot(spread, root_ref[g * narrow : (g + 1) * narrow, :], preferred_element_type=F32).astype(BF16)
        for h in range(width // narrow):
            cell = lax.dot_general(
                rows[:, h * narrow : (h + 1) * narrow], spread, (((1,), (1,)), ((), ())), preferred_element_type=F32
            )
            padded_ref[g * wide : (g + 1) * wide, h * wide : (h + 1) * wide] = cell.astype(BF16)
    left0_copy.wait()


def take_matrix(part):
    free = LANES - part
    shape = ((LANES // free) * LANES, LANES)
    row = lax.broadcasted_iota(jnp.int32, shape, 0)
    col = lax.broadcasted_iota(jnp.int32, shape, 1)
    return jnp.where((row // LANES == col // free) & (row % LANES == part + col % free), 1.0, 0.0).astype(BF16)


def extract_kernel(arr_ref, roots_hbm, out_ref, tall_ref):
    row_groups, col_groups, height, _ = arr_ref.shape
    row_part = height - 8
    width = row_groups * row_part
    part = width // col_groups
    take = take_matrix(part)
    span = take.shape[0] // LANES
    for g in range(col_groups // span):
        tiles = [arr_ref[:, g * span + m, :row_part, :].reshape(width, LANES) for m in range(span)]
        cols = jnp.dot(jnp.concatenate(tiles, axis=1), take, preferred_element_type=F32)
        out_ref[:, g * LANES : (g + 1) * LANES] = cols.astype(BF16)
    low = [arr_ref[:, m, row_part:, :].astype(F32).reshape(8 * row_groups, LANES) for m in range(col_groups)]
    low = swap_groups(low, LANES // col_groups)
    for k in range(row_part // 8):
        tall_ref[:, k] = low[k].reshape(row_groups, 8, LANES)
    out_ref[:, width // 2 - LANES :] = tall_ref[...].reshape(width, LANES).astype(BF16)


def first_kernel(arr_ref, left_ref, right_ref, out_hbm, wide_ref, out_ref, out_sems):
    row_groups, col_groups, row_part, _ = out_ref.shape
    for a in range(row_groups):
        for m in range(col_groups):
            wide_ref[a * row_part : (a + 1) * row_part, m * LANES : (m + 1) * LANES] = arr_ref[a, m, :row_part, :]
    stores = []
    start = 0
    for i, span in enumerate(FIRST_SPANS):
        left = left_ref[start * row_part : (start + span) * row_part, :]
        half = jnp.dot(left, wide_ref[...], preferred_element_type=F32).astype(BF16)
        result = jnp.dot(half, right_ref[...], preferred_element_type=F32).astype(BF16)
        for k in range(span):
            for m in range(col_groups):
                out_ref[start + k, m] = result[k * row_part : (k + 1) * row_part, m * LANES : (m + 1) * LANES]
        rows = pl.ds(start, span)
        stores.append(copy_in(out_ref.at[rows], out_hbm.at[rows, :, pl.ds(0, row_part), :], out_sems.at[i]))
        start += span
    for store in stores:
        store.wait()


def extra_kernel(
    mine_ref, other_ref, left_ref, picked_ref, first_hbm, out_hbm, block_hbm, message_ref, block_ref, top_ref, load_sems,
    store_sems, block_sem,
):
    row_groups, col_groups, height, _ = message_ref.shape
    row_part = height - 8
    width = left_ref.shape[0]
    half = width // 2
    groups = row_part // 8
    core = lax.axis_index("mp") % 2
    loads = []
    start = 0
    for i, span in enumerate(SPANS):
        rows = pl.ds(start, span)
        loads.append(copy_in(first_hbm.at[rows], message_ref.at[rows], load_sems.at[i]))
        start += span
    for j in range(2):

        @pl.when(core == j)
        def _(j=j):
            block_ref[:, j * half : (j + 1) * half] = mine_ref[...]
            block_ref[:, (1 - j) * half : (2 - j) * half] = other_ref[...]

    block_copy = copy_in(block_ref, block_hbm, block_sem)
    take = take_matrix(width // col_groups)
    wide = take.shape[0]
    transposed = (((1,), (1,)), ((), ()))
    stores = []
    start = 0
    for i, span in enumerate(SPANS):
        left = left_ref[start * row_part : (start + span) * row_part, :]
        temp = jnp.dot(left, block_ref[...], preferred_element_type=F32).astype(BF16)
        result = jnp.dot(temp, picked_ref[...], preferred_element_type=F32)
        top = result[:, : half - LANES].astype(BF16)
        for g in range(col_groups * LANES // wide):
            spread = lax.dot_general(top[:, g * LANES : (g + 1) * LANES], take, transposed, preferred_element_type=F32)
            top_ref[: span * row_part, g * wide : (g + 1) * wide] = spread.astype(BF16)
        rows = result[:, half - LANES :].reshape(span, groups, 8, LANES)
        low = [rows[:, k].reshape(8 * span, LANES) for k in range(groups)]
        low += [jnp.zeros((8 * span, LANES), F32)] * (col_groups - groups)
        low = swap_groups(low, LANES // col_groups)
        loads[i].wait()
        for k in range(span):
            for m in range(col_groups):
                cols = slice(m * LANES, (m + 1) * LANES)
                message_ref[start + k, m, :row_part] += top_ref[k * row_part : (k + 1) * row_part, cols]
                message_ref[start + k, m, row_part:] = low[m][8 * k : 8 * k + 8].astype(BF16)
        rows = pl.ds(start, span)
        stores.append(copy_in(message_ref.at[rows], out_hbm.at[rows], store_sems.at[i]))
        start += span
    for store in stores:
        store.wait()
    block_copy.wait()


def pair_gram_kernel(table_ref, arr_ref, halves_ref, left_ref, right_ref, left_out, right_out, wide_ref, block_ref):
    width = block_ref.shape[0]
    row_groups, col_groups, height, _ = arr_ref.shape
    row_part = width // row_groups
    part = width // col_groups
    tile = left_ref.shape[1]
    slot = pl.program_id(0)
    step = pl.program_id(1)
    has_extra = table_ref[table_ref.shape[0] - LANES + 2]

    @pl.when((step == 0) & (slot == 0))
    def _():
        for a in range(row_groups):
            for m in range(col_groups):
                wide_ref[a * row_part : (a + 1) * row_part, m * LANES : (m + 1) * LANES] = arr_ref[a, m][:row_part]
        spread = spread_matrix(part, LANES // (LANES - part))
        wide, narrow = spread.shape
        for g in range(width // narrow):
            cols = jnp.dot(wide_ref[:, g * wide : (g + 1) * wide], spread, preferred_element_type=F32)
            block_ref[:, g * narrow : (g + 1) * narrow] = cols.astype(BF16)

    @pl.when((step == 0) & (slot == 1) & (has_extra == 1))
    def _():
        half = width // 2
        total = jnp.zeros((width, width), F32)
        for j in range(2):
            order = halves_order((half, width), j, 0, part, col_groups)
            theirs = jnp.where(order == lax.broadcasted_iota(jnp.int32, (half, width), 1), 1.0, 0.0).astype(BF16)
            total += jnp.dot(halves_ref[:, j * half : (j + 1) * half], theirs, preferred_element_type=F32)
        block_ref[...] = total.astype(BF16)

    @pl.when((step == 0) & (slot == 1) & (has_extra == 0))
    def _():
        block_ref[...] = jnp.zeros_like(block_ref)

    for i in range(width // tile):

        @pl.when(step == i)
        def _(i=i):
            mine = slice(i * tile, (i + 1) * tile)
            left = lax.dot_general(
                block_ref[mine, :], block_ref[...], (((1,), (1,)), ((), ())), preferred_element_type=F32
            )
            left_out[0] = STAT_DECAY * left_ref[0] + (1.0 - STAT_DECAY) * left
            right = lax.dot_general(
                block_ref[:, mine], block_ref[...], (((0,), (0,)), ((), ())), preferred_element_type=F32
            )
            right_out[0] = STAT_DECAY * right_ref[0] + (1.0 - STAT_DECAY) * right


def exchange(x):
    return lax.all_to_all(x, ("dp", "mp"), split_axis=0, concat_axis=0, tiled=True)


def other_core(x):
    count = lax.axis_size("mp")
    return lax.ppermute(x, "mp", [(i, i ^ 1) for i in range(count)])


def pair_path(outgoing, table, gradient, owner, left_stat, right_stat, left_root, right_root):
    row_blocks, row_part, col_blocks, col_part = gradient.shape
    dp_count = lax.axis_size("dp")
    mp_count = lax.axis_size("mp")
    devices = dp_count * mp_count
    slots, width = left_stat.shape[2:4]
    wide = mp_count * LANES
    height = outgoing.shape[1]
    groups = row_part // 8
    pieces = 4
    smem = pl.BlockSpec(memory_space=pltpu.SMEM)
    vmem = pl.BlockSpec(memory_space=pltpu.VMEM)
    hbm = pl.BlockSpec(memory_space=HBM)
    dma = pltpu.SemaphoreType.DMA
    message_shape = (dp_count, mp_count, height, LANES)
    left_root = left_root[0, 0]
    right_root = right_root[0, 0]

    def params(mib):
        return pltpu.CompilerParams(vmem_limit_bytes=mib * MIB)

    def cost(flops, moved):
        return pl.CostEstimate(flops=int(flops * 1e9), bytes_accessed=int(moved * 1e6), transcendentals=0)

    def in_hbm(x):
        return pltpu.with_memory_space_constraint(x, HBM)

    arrived = exchange(outgoing).reshape(message_shape)
    padded, picked, left0, left1 = pl.pallas_call(
        prepare_kernel,
        out_shape=[
            HBM((wide, wide), BF16),
            HBM((width, width // 2), BF16),
            HBM((width, width), BF16),
            HBM((width, width), BF16),
        ],
        in_specs=[smem, hbm, hbm, hbm, hbm],
        out_specs=[vmem] * 4,
        scratch_shapes=[pltpu.VMEM((width, width), BF16), pltpu.VMEM((width, width), BF16), dma((4,))],
        cost_estimate=cost(6, 9),
        compiler_params=params(24),
        name="prepare_roots",
    )(table, left_root, right_root, other_core(left_root), other_core(right_root))
    mine = pl.pallas_call(
        extract_kernel,
        out_shape=jax.ShapeDtypeStruct((width, width // 2), BF16),
        in_specs=[vmem, hbm],
        out_specs=vmem,
        scratch_shapes=[pltpu.VMEM((dp_count, groups, 8, LANES), F32)],
        cost_estimate=cost(0.6, 3),
        compiler_params=params(16),
        name="extract_extra",
    )(arrived, in_hbm(left1))
    other = other_core(mine)
    first = pl.pallas_call(
        first_kernel,
        out_shape=HBM(message_shape, BF16),
        in_specs=[vmem, vmem, vmem],
        out_specs=hbm,
        scratch_shapes=[
            pltpu.VMEM((width, wide), BF16),
            pltpu.VMEM((dp_count, mp_count, row_part, LANES), BF16),
            dma((len(FIRST_SPANS),)),
        ],
        cost_estimate=cost(4, 9),
        compiler_params=params(20),
        name="precondition_first",
    )(arrived, left0, padded)
    leaving, halves = pl.pallas_call(
        extra_kernel,
        out_shape=[HBM(message_shape, BF16), HBM((width, width), BF16)],
        in_specs=[vmem] * 4 + [hbm],
        out_specs=[hbm, hbm],
        input_output_aliases={4: 0},
        scratch_shapes=[
            pltpu.VMEM(message_shape, BF16),
            pltpu.VMEM((width, width), BF16),
            pltpu.VMEM((max(SPANS) * row_part, wide), BF16),
            dma((len(SPANS),)),
            dma((len(SPANS),)),
            dma,
        ],
        cost_estimate=cost(3, 9),
        compiler_params=params(20),
        name="precondition_extra",
    )(mine, other, left1, picked, first)
    returned = exchange(leaving.reshape(outgoing.shape))
    tile = width // 3
    stat_spec = pl.BlockSpec((1, tile, width), lambda s, i: (s, i, 0))
    left_new, right_new = pl.pallas_call(
        pair_gram_kernel,
        grid=(slots, width // tile),
        out_shape=[jax.ShapeDtypeStruct((slots, width, width), F32)] * 2,
        in_specs=[
            smem,
            pl.BlockSpec(message_shape, lambda s, i: (0, 0, 0, 0)),
            pl.BlockSpec((width, width), lambda s, i: (0, 0)),
            stat_spec,
            stat_spec,
        ],
        out_specs=[stat_spec, stat_spec],
        scratch_shapes=[pltpu.VMEM((width, wide), BF16), pltpu.VMEM((width, width), BF16)],
        cost_estimate=cost(9, 25),
        compiler_params=params(24),
        name="pair_grams",
    )(table, in_hbm(arrived), halves, left_stat[0, 0], right_stat[0, 0])
    precond = pl.pallas_call(
        unpack_pairs_kernel,
        out_shape=HBM(gradient.shape, BF16),
        in_specs=[hbm, hbm, vmem],
        out_specs=hbm,
        scratch_shapes=[
            pltpu.SMEM(owner.shape, jnp.int32),
            pltpu.SMEM(table.shape, jnp.int32),
            pltpu.VMEM(gradient.shape, BF16),
            pltpu.VMEM((2, row_part * col_blocks, LANES), F32),
            dma((2,)),
            dma((pieces,)),
        ],
        compiler_params=params(12),
        name="unpack_pairs",
    )(in_hbm(owner), in_hbm(table), returned)
    return (precond, left_new[None, None], right_new[None, None])


def per_device(gradient, owner, left_stat, right_stat, left_root, right_root):
    row_blocks, row_part, col_blocks, col_part = gradient.shape
    devices = lax.axis_size("dp") * lax.axis_size("mp")
    height = row_part + 8
    hbm = pl.BlockSpec(memory_space=HBM)
    dma = pltpu.SemaphoreType.DMA
    outgoing, table, bad = pl.pallas_call(
        pack_pairs_kernel,
        out_shape=[
            HBM((devices, height, LANES), BF16),
            HBM((2 * devices + LANES,), jnp.int32),
            HBM((LANES,), jnp.int32),
        ],
        in_specs=[hbm, hbm],
        out_specs=[hbm, hbm, hbm],
        scratch_shapes=[
            pltpu.SMEM(owner.shape, jnp.int32),
            pltpu.VMEM(gradient.shape, BF16),
            pltpu.VMEM((devices, height, LANES), BF16),
            pltpu.VMEM(((row_blocks + 1) * row_part * col_blocks, LANES), F32),
            pltpu.SMEM((2 * devices + LANES,), jnp.int32),
            pltpu.SMEM((LANES,), jnp.int32),
            pltpu.SMEM((devices,), jnp.int32),
            pltpu.SMEM((devices + 1,), jnp.int32),
            pltpu.SMEM((devices,), jnp.int32),
            dma((4,)),
            dma((4,)),
            dma((3,)),
        ],
        compiler_params=pltpu.CompilerParams(vmem_limit_bytes=16 * MIB),
        name="pack_pairs",
    )(owner, gradient)
    rest = (gradient, owner, left_stat, right_stat, left_root, right_root)
    if not FALLBACK:
        return pair_path(outgoing, table, *rest)
    return lax.cond(bad[0] == 0, pair_path, lambda outgoing, table, *rest: general_path(*rest), outgoing, table, *rest)


def solution(mesh):
    return jax.shard_map(
        per_device,
        mesh=mesh,
        in_specs=(
            P(None, "dp", None, "mp"),
            P(),
            P("dp", "mp", None, None, None),
            P("dp", "mp", None, None, None),
            P("dp", "mp", None, None, None),
            P("dp", "mp", None, None, None),
        ),
        out_specs=(
            P(None, "dp", None, "mp"),
            P("dp", "mp", None, None, None),
            P("dp", "mp", None, None, None),
        ),
        check_vma=False,
    )
```

time: 158 us -> 91.2 us (0.58)
  local copies, waits for them, and re-layouts: 66.8 us -> 0.69 us
  Pallas kernels: 0 us -> 36 us
  matrix products: 33.6 us -> 0 us
  other arithmetic: 13 us -> 0 us
  waiting for transfers between devices: 25.2 us -> 34.6 us
    mul x4 -> x0, local copies, waits for them, and re-layouts: 40 us -> none  [the longest x2 25.1 us: per_device(): left_new = stat_decay * left_stat[0, 0] + (1.0 - stat_decay) * left_gram]
    pallas_call x0 -> x7, Pallas kernels: none -> 36 us  [the longest x1 12.2 us: pair_path(): pl.pallas_call(pair_gram_kernel, grid=(slots, width // tile), out_shape=[...]
    dot_general x5 -> x0, matrix products: 33.6 us -> none  [the longest x1 11.5 us: per_device(): jnp.einsum('amspq,bmsuq->sapbu', arrived, arrived, preferred_element_type...]
    another operation x2 -> x0, local copies, waits for them, and re-layouts: 16.4 us -> none  [the longest x1 9.98 us: per_device(): left_root[0, 0].reshape(slots, dp_count, row_part, dp_count, row_part)]
    add x2 -> x0, other arithmetic: 12.1 us -> none  [the longest x1 11.4 us: per_device(): right_new = stat_decay * right_stat[0, 0] + (1.0 - stat_decay) * right_gram]
    all_to_all x2, waiting for transfers between devices: 25.2 us -> 34.6 us  [exchange(): lax.all_to_all(x, ('dp', 'mp'), split_axis=0, concat_axis=0, tiled=True)]
    convert_element_type x1 -> x0, local copies, waits for them, and re-layouts: 4.65 us -> none  [per_device(): outgoing = jnp.einsum('rcd,rpcq->dpq', table, gradient, preferred_element...]
    reshape x1 -> x0, local copies, waits for them, and re-layouts: 4.06 us -> none  [per_device(): leaving.reshape(devices, slots, row_part, col_part)]
  transfers between devices with their start and end apart: 2 -> 5, of which waited for: 1 -> 2; matrix products, arithmetic and copies ran while one was open for 54% -> 0% of each run, Pallas kernels for 0% -> 27%
where the time goes in v1:
time: 91.2 us; the launch traced here: 90.7 us
  Pallas kernels  36 us (39%)
  waiting for transfers between devices  34.6 us (38%)
  starting transfers between devices  17.6 us (19%)
  between operations  1.49 us (2%)
    all_to_all x2, waiting for transfers between devices, exchange(): lax.all_to_all(x, ('dp', 'mp'), split_axis=0, concat_axis=0, tiled=True)  34.6 us
    all_to_all x2, starting transfers between devices, exchange(): lax.all_to_all(x, ('dp', 'mp'), split_axis=0, concat_axis=0, tiled=True)  15 us
    pallas_call x1, Pallas kernels, pair_path(): pl.pallas_call(pair_gram_kernel, grid=(slots, width // tile), out_shape=[...  12.2 us
    pallas_call x1, Pallas kernels, pair_path(): pl.pallas_call(prepare_kernel, out_shape=[HBM((wide, wide), BF16), HBM((w...  8.7 us
    pallas_call x1, Pallas kernels, pair_path(): pl.pallas_call(extra_kernel, out_shape=[HBM(message_shape, BF16), HBM((wi...  4 us
    pallas_call x1, Pallas kernels, pair_path(): pl.pallas_call(first_kernel, out_shape=HBM(message_shape, BF16), in_specs...  3.97 us
    pallas_call x1, Pallas kernels, per_device(): pl.pallas_call(pack_pairs_kernel, out_shape=[HBM((devices, height, LANES)...  3.91 us
    pallas_call x1, Pallas kernels, pair_path(): pl.pallas_call(unpack_pairs_kernel, out_shape=HBM(gradient.shape, BF16),...  2.59 us
  transfers between devices with their start and end apart: 5, of which 2 were waited for; matrix products, arithmetic and copies ran while one was open for 0% of the time, Pallas kernels for 27%

profile of v1, /device:TPU:1, one launch (start us, length us, event | category | flops | bytes accessed | tf_op | source)
XLA Modules:
  0.0 90.7 jit_solution(15492625130862943045)
XLA Ops:
  0.6 3.9 %pack_pairs.1 = (bf16[128,56,128]{2,1,0:T(8,128)(2,1)}, s32[384]{0:T(512)}, s32[128]{0:T(128)}) custom-call(s32[128]{0:T(128)} %owner_hbm.1, bf16[16,48,8,96]{3,2,1,0:T(8,128)(2,1)} %grad_hbm.1), custom_call_target="tpu_custom_call" | custom-call | tf_op jit(solution)/shard_map/pack_pairs/pallas_call | solution.py:777
  5.2 85.3 %conditional.1 = (bf16[16,48,8,96]{3,2,1,0:T(8,128)(2,1)}, f32[1,1,2,768,768]{4,3,2,1,0:T(8,128)}, f32[1,1,2,768,768]{4,3,2,1,0:T(8,128)}) conditional(s32[]{:T(128)} %bitcast.16, (s32[128]{0:T(128)}, bf16[16,48,8,96]{3,2,1,0:T(8,128)(2,1)}, bf16[1,1,2,768,768]{4,3,2,1,0:T(8,128)(2,1)}, bf16[1,1,2,768,768]{4,3,2,1,0:T(8,128)(2,1)}, ...), branch_computations={%region_0.0_spmd, %region_1.0_spmd} | conditional | flops 22599999488 | bytes 132179840 | solution.py:806
  5.2 0.0 copy-start.12
  5.2 1.5 %collective-permute-start = (bf16[2,768,768]{2,1,0:T(8,128)(2,1)}, bf16[2,768,768]{2,1,0:T(8,128)(2,1)}, u32[]{:S(2)}, u32[]{:S(2)}) collective-permute-start(bf16[2,768,768]{2,1,0:T(8,128)(2,1)} %bitcast.30), channel_id=1, source_target_pairs={{0,1},{1,0},{2,3},{3,2},{4,5},{5,4},{6,7},{7,6},{8,9},{9,8},{10,11... | collective-permute-start | bytes 7077896 | tf_op jit(solution)/shard_map/cond/branch_1_fun/ppermute | solution.py:643
  6.7 0.1 collective-permute-start.1
  6.8 10.5 %all-to-all-start.2 = ((bf16[128,56,128]{2,1,0:T(8,128)(2,1)}), bf16[128,56,128]{2,1,0:T(8,128)(2,1)S(1)}, u32[]{:S(2)}, u32[]{:S(2)}) async-start(bf16[128,56,128]{2,1,0:T(8,128)(2,1)} %get-tuple-element.36), calls=%async_computation.2 | async-start | bytes 3670016 | tf_op jit(solution)/shard_map/cond/branch_1_fun/all_to_all | solution.py:638
  17.3 0.0 collective-permute-done.left_other_hbm
  17.3 0.0 collective-permute-done.1.right_other_hbm
  17.4 0.0 copy-done.12
  17.4 8.7 %prepare_roots.1 = (bf16[1024,1024]{1,0:T(8,128)(2,1)}, bf16[768,384]{1,0:T(8,128)(2,1)}, bf16[768,768]{1,0:T(8,128)(2,1)}, bf16[768,768]{1,0:T(8,128)(2,1)}) custom-call(s32[384]{0:T(512)S(1)} %copy-done.12, bf16[2,768,768]{2,1,0:T(8,128)(2,1)} %bitcast.31, bf16[2,768,768]{2,1,0:T(8,128)(2,1)} %bitcast.34, ...), custom_call_target="tpu_custom_call" | custom-call | flops 6000000000 | bytes 9000000 | tf_op jit(solution)/shard_map/cond/branch_1_fun/prepare_roots/pallas_call | solution.py:674
  26.1 0.0 copy-start.9
  26.1 19.0 %all-to-all-done.2 = bf16[128,56,128]{2,1,0:T(8,128)(2,1)S(1)} async-done(((bf16[128,56,128]{2,1,0:T(8,128)(2,1)}), bf16[128,56,128]{2,1,0:T(8,128)(2,1)S(1)}, u32[]{:S(2)}, u32[]{:S(2)}) %all-to-all-start.2) | async-done | bytes 1835040 | tf_op jit(solution)/shard_map/cond/branch_1_fun/all_to_all | solution.py:638
  45.0 0.0 copy-start
  45.0 0.0 copy-start.7
  45.0 0.6 extract_extra.1.mine_ref
  45.6 1.0 %collective-permute-start.2 = (bf16[768,384]{1,0:T(8,128)(2,1)S(1)}, bf16[768,384]{1,0:T(8,128)(2,1)S(1)}, u32[]{:S(2)}, u32[]{:S(2)}) collective-permute-start(bf16[768,384]{1,0:T(8,128)(2,1)S(1)} %extract_extra.1.mine_ref), channel_id=1, source_target_pairs={{0,1},{1,0},{2,3},{3,2},{4,5},{5,4},{6,7},{7,6},{8,9},{9,8},{10,11... | collective-permute-start | bytes 1769480 | tf_op jit(solution)/shard_map/cond/branch_1_fun/ppermute | solution.py:643
  46.6 0.0 copy-done.9
  46.6 0.7 copy-done.7
  47.3 0.0 copy-start.4
  47.3 0.0 copy-start.10
  47.3 4.0 %precondition_first.1.first_hbm = bf16[16,8,56,128]{3,2,1,0:T(8,128)(2,1)} custom-call(bf16[16,8,56,128]{3,2,1,0:T(8,128)(2,1)S(1)} %bitcast.19, bf16[768,768]{1,0:T(8,128)(2,1)S(1)} %copy-done.9, bf16[1024,1024]{1,0:T(8,128)(2,1)S(1)} %copy-done.7), custom_call_target="tpu_custom_call" | custom-call | flops 4000000000 | bytes 9000000 | tf_op jit(solution)/shard_map/cond/branch_1_fun/precondition_first/pallas_call | solution.py:700
  51.3 0.0 copy-done
  51.3 0.0 collective-permute-done.2.other_ref
  51.3 0.0 copy-done.4
  51.3 0.0 copy-done.10
  51.3 4.0 %precondition_extra.1 = (bf16[16,8,56,128]{3,2,1,0:T(8,128)(2,1)}, bf16[768,768]{1,0:T(8,128)(2,1)}) custom-call(bf16[768,384]{1,0:T(8,128)(2,1)S(1)} %extract_extra.1.mine_ref, bf16[768,384]{1,0:T(8,128)(2,1)S(1)} %collective-permute-done.2.other_ref, bf16[768,768]{1,0:T(8,128)(2,1)S(1)} %copy-done.4, ...), custom_call_target="tpu_custom_call", output_to_operand_aliasing={{0}: (4, {})} | custom-call | flops 3000000000 | bytes 9000000 | tf_op jit(solution)/shard_map/cond/branch_1_fun/precondition_extra/pallas_call | solution.py:714
  55.3 0.0 copy-start.8
  55.3 4.5 %all-to-all-start.3 = ((bf16[128,56,128]{2,1,0:T(8,128)(2,1)}), bf16[128,56,128]{2,1,0:T(8,128)(2,1)S(1)}, u32[]{:S(2)}, u32[]{:S(2)}) async-start(bf16[128,56,128]{2,1,0:T(8,128)(2,1)} %bitcast.24), calls=%async_computation.3 | async-start | bytes 3670016 | tf_op jit(solution)/shard_map/cond/branch_1_fun/all_to_all | solution.py:638
  59.8 0.0 copy-done.8
  59.9 12.2 %pair_grams.1 = (f32[2,768,768]{2,1,0:T(8,128)}, f32[2,768,768]{2,1,0:T(8,128)}) custom-call(s32[384]{0:T(512)S(1)} %copy-done.12, bf16[16,8,56,128]{3,2,1,0:T(8,128)(2,1)} %bitcast.20, bf16[768,768]{1,0:T(8,128)(2,1)S(1)} %copy-done.8, f32[2,768,768]{2,1,0:T(8,128)} %bitcast.26, f32[2,768,768]{2,1,0:T(8,128)} %bitcast.28), custom_call_target="tpu_custom_call" | custom-call | flops 8999999488 | bytes 25000000 | tf_op jit(solution)/shard_map/cond/branch_1_fun/pair_grams/pallas_call | solution.py:735
  72.0 15.7 %all-to-all-done.3.back_ref = bf16[128,56,128]{2,1,0:T(8,128)(2,1)S(1)} async-done(((bf16[128,56,128]{2,1,0:T(8,128)(2,1)}), bf16[128,56,128]{2,1,0:T(8,128)(2,1)S(1)}, u32[]{:S(2)}, u32[]{:S(2)}) %all-to-all-start.3) | async-done | bytes 1835040 | tf_op jit(solution)/shard_map/cond/branch_1_fun/all_to_all | solution.py:638
  87.7 2.6 %unpack_pairs.1 = bf16[16,48,8,96]{3,2,1,0:T(8,128)(2,1)} custom-call(s32[128]{0:T(128)} %get-tuple-element.34.owner_hbm, s32[384]{0:T(512)} %get-tuple-element.35.table_ref.table_hbm, bf16[128,56,128]{2,1,0:T(8,128)(2,1)S(1)} %all-to-all-done.3.back_ref), custom_call_target="tpu_custom_call" | custom-call | tf_op jit(solution)/shard_map/cond/branch_1_fun/unpack_pairs/pallas_call | solution.py:752
Async XLA Ops:
  5.2 12.1 %copy-start.12 = (s32[384]{0:T(512)S(1)}, s32[384]{0:T(512)}, u32[]{:S(2)}) copy-start(s32[384]{0:T(512)} %get-tuple-element.35.table_ref.table_hbm) | copy-start | bytes 4612 | tf_op jit(solution)/shard_map/cond
  5.2 12.1 %collective-permute-start = (bf16[2,768,768]{2,1,0:T(8,128)(2,1)}, bf16[2,768,768]{2,1,0:T(8,128)(2,1)}, u32[]{:S(2)}, u32[]{:S(2)}) collective-permute-start(bf16[2,768,768]{2,1,0:T(8,128)(2,1)} %bitcast.30), channel_id=1, source_target_pairs={{0,1},{1,0},{2,3},{3,2},{4,5},{5,4},{6,7},{7,6},{8,9},{9,8},{10,11... | collective-permute-start | bytes 7077896 | tf_op jit(solution)/shard_map/cond/branch_1_fun/ppermute | solution.py:643
  6.7 10.6 %collective-permute-start.1 = (bf16[2,768,768]{2,1,0:T(8,128)(2,1)}, bf16[2,768,768]{2,1,0:T(8,128)(2,1)}, u32[]{:S(2)}, u32[]{:S(2)}) collective-permute-start(bf16[2,768,768]{2,1,0:T(8,128)(2,1)} %bitcast.33), channel_id=1, source_target_pairs={{0,1},{1,0},{2,3},{3,2},{4,5},{5,4},{6,7},{7,6},{8,9},{9,8},{10,11... | collective-permute-start | bytes 7077896 | tf_op jit(solution)/shard_map/cond/branch_1_fun/ppermute | solution.py:643
  6.8 38.2 %all-to-all-start.2 = ((bf16[128,56,128]{2,1,0:T(8,128)(2,1)}), bf16[128,56,128]{2,1,0:T(8,128)(2,1)S(1)}, u32[]{:S(2)}, u32[]{:S(2)}) async-start(bf16[128,56,128]{2,1,0:T(8,128)(2,1)} %get-tuple-element.36), calls=%async_computation.2 | async-start | bytes 3670016 | tf_op jit(solution)/shard_map/cond/branch_1_fun/all_to_all | solution.py:638
  26.1 20.6 %copy-start.9 = (bf16[768,768]{1,0:T(8,128)(2,1)S(1)}, bf16[768,768]{1,0:T(8,128)(2,1)}, u32[]{:S(2)}) copy-start(bf16[768,768]{1,0:T(8,128)(2,1)} %get-tuple-element.41.left_ref) | copy-start | bytes 3538948 | tf_op jit(solution)/shard_map/cond
  45.0 6.2 %copy-start = (bf16[128,56,128]{2,1,0:T(8,128)(2,1)}, bf16[128,56,128]{2,1,0:T(8,128)(2,1)S(1)}, u32[]{:S(2)}) copy-start(bf16[128,56,128]{2,1,0:T(8,128)(2,1)S(1)} %all-to-all-done.2) | copy-start | bytes 5505028 | tf_op jit(solution)/shard_map/cond
  45.0 2.3 %copy-start.7 = (bf16[1024,1024]{1,0:T(8,128)(2,1)S(1)}, bf16[1024,1024]{1,0:T(8,128)(2,1)}, u32[]{:S(2)}) copy-start(bf16[1024,1024]{1,0:T(8,128)(2,1)} %get-tuple-element.42.right_ref) | copy-start | bytes 6291460 | tf_op jit(solution)/shard_map/cond
  45.6 5.6 %collective-permute-start.2 = (bf16[768,384]{1,0:T(8,128)(2,1)S(1)}, bf16[768,384]{1,0:T(8,128)(2,1)S(1)}, u32[]{:S(2)}, u32[]{:S(2)}) collective-permute-start(bf16[768,384]{1,0:T(8,128)(2,1)S(1)} %extract_extra.1.mine_ref), channel_id=1, source_target_pairs={{0,1},{1,0},{2,3},{3,2},{4,5},{5,4},{6,7},{7,6},{8,9},{9,8},{10,11... | collective-permute-start | bytes 1769480 | tf_op jit(solution)/shard_map/cond/branch_1_fun/ppermute | solution.py:643
  47.3 4.0 %copy-start.4 = (bf16[768,768]{1,0:T(8,128)(2,1)S(1)}, bf16[768,768]{1,0:T(8,128)(2,1)}, u32[]{:S(2)}) copy-start(bf16[768,768]{1,0:T(8,128)(2,1)} %get-tuple-element.39.roots_hbm.left_ref) | copy-start | bytes 3538948 | tf_op jit(solution)/shard_map/cond
  47.3 4.0 %copy-start.10 = (bf16[768,384]{1,0:T(8,128)(2,1)S(1)}, bf16[768,384]{1,0:T(8,128)(2,1)}, u32[]{:S(2)}) copy-start(bf16[768,384]{1,0:T(8,128)(2,1)} %get-tuple-element.40.picked_ref) | copy-start | bytes 1769476 | tf_op jit(solution)/shard_map/cond
  55.3 4.5 %copy-start.8 = (bf16[768,768]{1,0:T(8,128)(2,1)S(1)}, bf16[768,768]{1,0:T(8,128)(2,1)}, u32[]{:S(2)}) copy-start(bf16[768,768]{1,0:T(8,128)(2,1)} %get-tuple-element.44.halves_ref) | copy-start | bytes 3538948 | tf_op jit(solution)/shard_map/cond
  55.3 32.4 %all-to-all-start.3 = ((bf16[128,56,128]{2,1,0:T(8,128)(2,1)}), bf16[128,56,128]{2,1,0:T(8,128)(2,1)S(1)}, u32[]{:S(2)}, u32[]{:S(2)}) async-start(bf16[128,56,128]{2,1,0:T(8,128)(2,1)} %bitcast.24), calls=%async_computation.3 | async-start | bytes 3670016 | tf_op jit(solution)/shard_map/cond/branch_1_fun/all_to_all | solution.py:638

commit v2 on v1

--- a/solution.py
+++ b/solution.py
@@ -12,8 +12,7 @@
 MIB = 1024 * 1024
 FALLBACK = True
 HBM = pltpu.HBM
-FIRST_SPANS = (8, 4, 4)
-SPANS = (8, 8)
+SPANS = (8, 4, 4)
 
 
 def spread_matrix(part, groups):
@@ -308,8 +307,9 @@
         return carry
 
     stores = []
-    share = devices // chunks
-    for i in range(chunks):
+    pieces = store_sems.shape[0]
+    share = devices // pieces
+    for i in range(pieces):
         lax.fori_loop(i * share, (i + 1) * share, message, 0, unroll=8)
 
         def extra(e, carry, i=i):
@@ -508,43 +508,32 @@
     out_ref[:, width // 2 - LANES :] = tall_ref[...].reshape(width, LANES).astype(BF16)
 
 
-def first_kernel(arr_ref, left_ref, right_ref, out_hbm, wide_ref, out_ref, out_sems):
-    row_groups, col_groups, row_part, _ = out_ref.shape
+def half_kernel(arr_ref, left_ref, half_ref, wide_hbm, wide_ref, sem):
+    row_groups, col_groups, height, _ = arr_ref.shape
+    row_part = height - 8
     for a in range(row_groups):
         for m in range(col_groups):
             wide_ref[a * row_part : (a + 1) * row_part, m * LANES : (m + 1) * LANES] = arr_ref[a, m, :row_part, :]
-    stores = []
-    start = 0
-    for i, span in enumerate(FIRST_SPANS):
-        left = left_ref[start * row_part : (start + span) * row_part, :]
-        half = jnp.dot(left, wide_ref[...], preferred_element_type=F32).astype(BF16)
-        result = jnp.dot(half, right_ref[...], preferred_element_type=F32).astype(BF16)
-        for k in range(span):
-            for m in range(col_groups):
-                out_ref[start + k, m] = result[k * row_part : (k + 1) * row_part, m * LANES : (m + 1) * LANES]
-        rows = pl.ds(start, span)
-        stores.append(copy_in(out_ref.at[rows], out_hbm.at[rows, :, pl.ds(0, row_part), :], out_sems.at[i]))
-        start += span
-    for store in stores:
-        store.wait()
-
-
-def extra_kernel(
-    mine_ref, other_ref, left_ref, picked_ref, first_hbm, out_hbm, block_hbm, message_ref, block_ref, top_ref, load_sems,
-    store_sems, block_sem,
+    wide_copy = copy_in(wide_ref, wide_hbm, sem)
+    step = left_ref.shape[0] // 2
+    for i in range(2):
+        rows = slice(i * step, (i + 1) * step)
+        half_ref[rows, :] = jnp.dot(left_ref[rows, :], wide_ref[...], preferred_element_type=F32).astype(BF16)
+    wide_copy.wait()
+
+
+def products_kernel(
+    half_ref, right0_ref, mine_ref, other_ref, left1_hbm, right1_hbm, out_hbm, block_hbm, block_ref, left1_ref, right1_ref, top_ref,
+    message_ref, store_sems, sems,
 ):
     row_groups, col_groups, height, _ = message_ref.shape
     row_part = height - 8
-    width = left_ref.shape[0]
+    width = left1_ref.shape[0]
     half = width // 2
     groups = row_part // 8
     core = lax.axis_index("mp") % 2
-    loads = []
-    start = 0
-    for i, span in enumerate(SPANS):
-        rows = pl.ds(start, span)
-        loads.append(copy_in(first_hbm.at[rows], message_ref.at[rows], load_sems.at[i]))
-        start += span
+    left1_copy = copy_in(left1_hbm, left1_ref, sems.at[0])
+    right1_copy = copy_in(right1_hbm, right1_ref, sems.at[1])
     for j in range(2):
 
         @pl.when(core == j)
@@ -552,42 +541,47 @@
             block_ref[:, j * half : (j + 1) * half] = mine_ref[...]
             block_ref[:, (1 - j) * half : (2 - j) * half] = other_ref[...]
 
-    block_copy = copy_in(block_ref, block_hbm, block_sem)
+    block_copy = copy_in(block_ref, block_hbm, sems.at[2])
     take = take_matrix(width // col_groups)
     wide = take.shape[0]
     transposed = (((1,), (1,)), ((), ()))
     stores = []
     start = 0
     for i, span in enumerate(SPANS):
-        left = left_ref[start * row_part : (start + span) * row_part, :]
-        temp = jnp.dot(left, block_ref[...], preferred_element_type=F32).astype(BF16)
-        result = jnp.dot(temp, picked_ref[...], preferred_element_type=F32)
-        top = result[:, : half - LANES].astype(BF16)
+        rows = slice(start * row_part, (start + span) * row_part)
+        first = jnp.dot(half_ref[rows, :], right0_ref[...], preferred_element_type=F32).astype(BF16)
+        for k in range(span):
+            for m in range(col_groups):
+                message_ref[start + k, m, :row_part] = first[k * row_part : (k + 1) * row_part, m * LANES : (m + 1) * LANES]
+        if i == 0:
+            left1_copy.wait()
+            right1_copy.wait()
+        temp = jnp.dot(left1_ref[rows, :], block_ref[...], preferred_element_type=F32).astype(BF16)
+        extra = jnp.dot(temp, right1_ref[...], preferred_element_type=F32)
+        top = extra[:, : half - LANES].astype(BF16)
         for g in range(col_groups * LANES // wide):
             spread = lax.dot_general(top[:, g * LANES : (g + 1) * LANES], take, transposed, preferred_element_type=F32)
             top_ref[: span * row_part, g * wide : (g + 1) * wide] = spread.astype(BF16)
-        rows = result[:, half - LANES :].reshape(span, groups, 8, LANES)
-        low = [rows[:, k].reshape(8 * span, LANES) for k in range(groups)]
+        low = extra[:, half - LANES :].reshape(span, groups, 8, LANES)
+        low = [low[:, k].reshape(8 * span, LANES) for k in range(groups)]
         low += [jnp.zeros((8 * span, LANES), F32)] * (col_groups - groups)
         low = swap_groups(low, LANES // col_groups)
-        loads[i].wait()
         for k in range(span):
             for m in range(col_groups):
                 cols = slice(m * LANES, (m + 1) * LANES)
                 message_ref[start + k, m, :row_part] += top_ref[k * row_part : (k + 1) * row_part, cols]
                 message_ref[start + k, m, row_part:] = low[m][8 * k : 8 * k + 8].astype(BF16)
-        rows = pl.ds(start, span)
-        stores.append(copy_in(message_ref.at[rows], out_hbm.at[rows], store_sems.at[i]))
+        part = pl.ds(start, span)
+        stores.append(copy_in(message_ref.at[part], out_hbm.at[part], store_sems.at[i]))
         start += span
+    block_copy.wait()
     for store in stores:
         store.wait()
-    block_copy.wait()
-
-
-def pair_gram_kernel(table_ref, arr_ref, halves_ref, left_ref, right_ref, left_out, right_out, wide_ref, block_ref):
+
+
+def pair_gram_kernel(table_ref, wide_ref, halves_ref, left_ref, right_ref, left_out, right_out, block_ref):
     width = block_ref.shape[0]
-    row_groups, col_groups, height, _ = arr_ref.shape
-    row_part = width // row_groups
+    col_groups = wide_ref.shape[1] // LANES
     part = width // col_groups
     tile = left_ref.shape[1]
     slot = pl.program_id(0)
@@ -596,9 +590,6 @@
 
     @pl.when((step == 0) & (slot == 0))
     def _():
-        for a in range(row_groups):
-            for m in range(col_groups):
-                wide_ref[a * row_part : (a + 1) * row_part, m * LANES : (m + 1) * LANES] = arr_ref[a, m][:row_part]
         spread = spread_matrix(part, LANES // (LANES - part))
         wide, narrow = spread.shape
         for g in range(width // narrow):
@@ -697,38 +688,34 @@
         name="extract_extra",
     )(arrived, in_hbm(left1))
     other = other_core(mine)
-    first = pl.pallas_call(
-        first_kernel,
-        out_shape=HBM(message_shape, BF16),
-        in_specs=[vmem, vmem, vmem],
-        out_specs=hbm,
+    half, block = pl.pallas_call(
+        half_kernel,
+        out_shape=[pltpu.VMEM((width, wide), BF16), HBM((width, wide), BF16)],
+        in_specs=[vmem, vmem],
+        out_specs=[vmem, hbm],
+        scratch_shapes=[pltpu.VMEM((width, wide), BF16), dma],
+        cost_estimate=cost(2, 6),
+        compiler_params=params(16),
+        name="half_product",
+    )(arrived, left0)
+    leaving, halves = pl.pallas_call(
+        products_kernel,
+        out_shape=[HBM(message_shape, BF16), HBM((width, width), BF16)],
+        in_specs=[vmem] * 4 + [hbm] * 2,
+        out_specs=[hbm] * 2,
         scratch_shapes=[
-            pltpu.VMEM((width, wide), BF16),
-            pltpu.VMEM((dp_count, mp_count, row_part, LANES), BF16),
-            dma((len(FIRST_SPANS),)),
+            pltpu.VMEM((width, width), BF16),
+            pltpu.VMEM((width, width), BF16),
+            pltpu.VMEM((width, width // 2), BF16),
+            pltpu.VMEM((max(SPANS) * row_part, wide), BF16),
+            pltpu.VMEM(message_shape, BF16),
+            dma((len(SPANS),)),
+            dma((3,)),
         ],
-        cost_estimate=cost(4, 9),
-        compiler_params=params(20),
-        name="precondition_first",
-    )(arrived, left0, padded)
-    leaving, halves = pl.pallas_call(
-        extra_kernel,
-        out_shape=[HBM(message_shape, BF16), HBM((width, width), BF16)],
-        in_specs=[vmem] * 4 + [hbm],
-        out_specs=[hbm, hbm],
-        input_output_aliases={4: 0},
-        scratch_shapes=[
-            pltpu.VMEM(message_shape, BF16),
-            pltpu.VMEM((width, width), BF16),
-            pltpu.VMEM((max(SPANS) * row_part, wide), BF16),
-            dma((len(SPANS),)),
-            dma((len(SPANS),)),
-            dma,
-        ],
-        cost_estimate=cost(3, 9),
-        compiler_params=params(20),
-        name="precondition_extra",
-    )(mine, other, left1, picked, first)
+        cost_estimate=cost(5, 12),
+        compiler_params=params(28),
+        name="precondition",
+    )(half, padded, mine, other, in_hbm(left1), in_hbm(picked))
     returned = exchange(leaving.reshape(outgoing.shape))
     tile = width // 3
     stat_spec = pl.BlockSpec((1, tile, width), lambda s, i: (s, i, 0))
@@ -738,17 +725,17 @@
         out_shape=[jax.ShapeDtypeStruct((slots, width, width), F32)] * 2,
         in_specs=[
             smem,
-            pl.BlockSpec(message_shape, lambda s, i: (0, 0, 0, 0)),
+            pl.BlockSpec((width, wide), lambda s, i: (0, 0)),
             pl.BlockSpec((width, width), lambda s, i: (0, 0)),
             stat_spec,
             stat_spec,
         ],
         out_specs=[stat_spec, stat_spec],
-        scratch_shapes=[pltpu.VMEM((width, wide), BF16), pltpu.VMEM((width, width), BF16)],
+        scratch_shapes=[pltpu.VMEM((width, width), BF16)],
         cost_estimate=cost(9, 25),
         compiler_params=params(24),
         name="pair_grams",
-    )(table, in_hbm(arrived), halves, left_stat[0, 0], right_stat[0, 0])
+    )(table, in_hbm(block), in_hbm(halves), left_stat[0, 0], right_stat[0, 0])
     precond = pl.pallas_call(
         unpack_pairs_kernel,
         out_shape=HBM(gradient.shape, BF16),
@@ -793,7 +780,7 @@
             pltpu.SMEM((devices,), jnp.int32),
             pltpu.SMEM((devices + 1,), jnp.int32),
             pltpu.SMEM((devices,), jnp.int32),
-            dma((4,)),
+            dma((2,)),
             dma((4,)),
             dma((3,)),
         ],

time: 91.2 us -> 90.1 us (0.988)
  transfers between devices with their start and end apart: 5 -> 5, of which waited for: 2 -> 2; matrix products, arithmetic and copies ran while one was open for 0% -> 0% of each run, Pallas kernels for 27% -> 26%
where the time goes in v2:
time: 90.1 us; the launch traced here: 89.6 us
  Pallas kernels  36.6 us (41%)
  waiting for transfers between devices  34.2 us (38%)
  starting transfers between devices  16.9 us (19%)
  between operations  1.49 us (2%)
    all_to_all x2, waiting for transfers between devices, exchange(): lax.all_to_all(x, ('dp', 'mp'), split_axis=0, concat_axis=0, tiled=True)  34.2 us
    all_to_all x2, starting transfers between devices, exchange(): lax.all_to_all(x, ('dp', 'mp'), split_axis=0, concat_axis=0, tiled=True)  14.3 us
    pallas_call x1, Pallas kernels, pair_path(): pl.pallas_call(pair_gram_kernel, grid=(slots, width // tile), out_shape=[...  12.4 us
    pallas_call x1, Pallas kernels, pair_path(): pl.pallas_call(prepare_kernel, out_shape=[HBM((wide, wide), BF16), HBM((w...  8.7 us
    pallas_call x1, Pallas kernels, pair_path(): pl.pallas_call(products_kernel, out_shape=[HBM(message_shape, BF16), HBM(...  6.5 us
    pallas_call x1, Pallas kernels, per_device(): pl.pallas_call(pack_pairs_kernel, out_shape=[HBM((devices, height, LANES)...  4.04 us
    pallas_call x1, Pallas kernels, pair_path(): pl.pallas_call(unpack_pairs_kernel, out_shape=HBM(gradient.shape, BF16),...  2.59 us
    ppermute x3, starting transfers between devices, other_core(): return lax.ppermute(x, 'mp', [(i, i ^ 1) for i in range(count)])  2.57 us
  transfers between devices with their start and end apart: 5, of which 2 were waited for; matrix products, arithmetic and copies ran while one was open for 0% of the time, Pallas kernels for 26%

profile of v2, /device:TPU:1, one launch (start us, length us, event | category | flops | bytes accessed | tf_op | source)
XLA Modules:
  0.0 89.6 jit_solution(10871752045112555525)
XLA Ops:
  0.6 4.0 %pack_pairs.1 = (bf16[128,56,128]{2,1,0:T(8,128)(2,1)}, s32[384]{0:T(512)}, s32[128]{0:T(128)}) custom-call(s32[128]{0:T(128)} %owner_hbm.1, bf16[16,48,8,96]{3,2,1,0:T(8,128)(2,1)} %grad_hbm.1), custom_call_target="tpu_custom_call" | custom-call | tf_op jit(solution)/shard_map/pack_pairs/pallas_call | solution.py:764
  5.3 84.1 %conditional.1 = (bf16[16,48,8,96]{3,2,1,0:T(8,128)(2,1)}, f32[1,1,2,768,768]{4,3,2,1,0:T(8,128)}, f32[1,1,2,768,768]{4,3,2,1,0:T(8,128)}) conditional(s32[]{:T(128)} %bitcast.16, (s32[128]{0:T(128)}, bf16[16,48,8,96]{3,2,1,0:T(8,128)(2,1)}, bf16[1,1,2,768,768]{4,3,2,1,0:T(8,128)(2,1)}, bf16[1,1,2,768,768]{4,3,2,1,0:T(8,128)(2,1)}, ...), branch_computations={%region_0.0_spmd, %region_1.0_spmd} | conditional | flops 22599999488 | bytes 132179840 | solution.py:793
  5.3 0.0 copy-start.8
  5.4 1.5 %collective-permute-start = (bf16[2,768,768]{2,1,0:T(8,128)(2,1)}, bf16[2,768,768]{2,1,0:T(8,128)(2,1)}, u32[]{:S(2)}, u32[]{:S(2)}) collective-permute-start(bf16[2,768,768]{2,1,0:T(8,128)(2,1)} %bitcast.29), channel_id=1, source_target_pairs={{0,1},{1,0},{2,3},{3,2},{4,5},{5,4},{6,7},{7,6},{8,9},{9,8},{10,11... | collective-permute-start | bytes 7077896 | tf_op jit(solution)/shard_map/cond/branch_1_fun/ppermute | solution.py:634
  6.9 0.1 collective-permute-start.1
  7.0 10.5 %all-to-all-start.2 = ((bf16[128,56,128]{2,1,0:T(8,128)(2,1)}), bf16[128,56,128]{2,1,0:T(8,128)(2,1)S(1)}, u32[]{:S(2)}, u32[]{:S(2)}) async-start(bf16[128,56,128]{2,1,0:T(8,128)(2,1)} %get-tuple-element.36), calls=%async_computation.2 | async-start | bytes 3670016 | tf_op jit(solution)/shard_map/cond/branch_1_fun/all_to_all | solution.py:629
  17.5 0.0 collective-permute-done.left_other_hbm
  17.5 0.0 collective-permute-done.1.right_other_hbm
  17.5 0.0 copy-done.8
  17.5 8.7 %prepare_roots.1 = (bf16[1024,1024]{1,0:T(8,128)(2,1)}, bf16[768,384]{1,0:T(8,128)(2,1)}, bf16[768,768]{1,0:T(8,128)(2,1)}, bf16[768,768]{1,0:T(8,128)(2,1)}) custom-call(s32[384]{0:T(512)S(1)} %copy-done.8, bf16[2,768,768]{2,1,0:T(8,128)(2,1)} %bitcast.30, bf16[2,768,768]{2,1,0:T(8,128)(2,1)} %bitcast.33, ...), custom_call_target="tpu_custom_call" | custom-call | flops 6000000000 | bytes 9000000 | tf_op jit(solution)/shard_map/cond/branch_1_fun/prepare_roots/pallas_call | solution.py:665
  26.2 0.0 copy-start.3
  26.2 19.0 %all-to-all-done.2 = bf16[128,56,128]{2,1,0:T(8,128)(2,1)S(1)} async-done(((bf16[128,56,128]{2,1,0:T(8,128)(2,1)}), bf16[128,56,128]{2,1,0:T(8,128)(2,1)S(1)}, u32[]{:S(2)}, u32[]{:S(2)}) %all-to-all-start.2) | async-done | bytes 1835040 | tf_op jit(solution)/shard_map/cond/branch_1_fun/all_to_all | solution.py:629
  45.2 0.6 extract_extra.1.mine_ref
  45.8 1.0 %collective-permute-start.2 = (bf16[768,384]{1,0:T(8,128)(2,1)S(1)}, bf16[768,384]{1,0:T(8,128)(2,1)S(1)}, u32[]{:S(2)}, u32[]{:S(2)}) collective-permute-start(bf16[768,384]{1,0:T(8,128)(2,1)S(1)} %extract_extra.1.mine_ref), channel_id=1, source_target_pairs={{0,1},{1,0},{2,3},{3,2},{4,5},{5,4},{6,7},{7,6},{8,9},{9,8},{10,11... | collective-permute-start | bytes 1769480 | tf_op jit(solution)/shard_map/cond/branch_1_fun/ppermute | solution.py:634
  46.8 0.0 copy-done.3
  46.8 0.0 copy-start.6
  46.8 1.8 %half_product.1 = (bf16[768,1024]{1,0:T(8,128)(2,1)S(1)}, bf16[768,1024]{1,0:T(8,128)(2,1)}) custom-call(bf16[16,8,56,128]{3,2,1,0:T(8,128)(2,1)S(1)} %bitcast.19, bf16[768,768]{1,0:T(8,128)(2,1)S(1)} %copy-done.3), custom_call_target="tpu_custom_call" | custom-call | flops 2000000000 | bytes 6000000 | tf_op jit(solution)/shard_map/cond/branch_1_fun/half_product/pallas_call | solution.py:691
  48.5 0.0 collective-permute-done.2.other_ref
  48.5 0.0 copy-done.6
  48.5 6.5 %precondition.3 = (bf16[16,8,56,128]{3,2,1,0:T(8,128)(2,1)}, bf16[768,768]{1,0:T(8,128)(2,1)}) custom-call(bf16[768,1024]{1,0:T(8,128)(2,1)S(1)} %get-tuple-element.40.half_ref, bf16[1024,1024]{1,0:T(8,128)(2,1)S(1)} %copy-done.6, bf16[768,384]{1,0:T(8,128)(2,1)S(1)} %extract_extra.1.mine_ref, bf16[768,384]{1,0:T(8,128)(2,1)S(1)} %collective-permute-done.2.other_ref, ...), custom_call_target="tpu_custom_call" | custom-call | flops 5000000000 | bytes 12000000 | tf_op jit(solution)/shard_map/cond/branch_1_fun/precondition/pallas_call | solution.py:701
  55.1 3.8 %all-to-all-start.3 = ((bf16[128,56,128]{2,1,0:T(8,128)(2,1)}), bf16[128,56,128]{2,1,0:T(8,128)(2,1)S(1)}, u32[]{:S(2)}, u32[]{:S(2)}) async-start(bf16[128,56,128]{2,1,0:T(8,128)(2,1)} %bitcast.23), calls=%async_computation.3 | async-start | bytes 3670016 | tf_op jit(solution)/shard_map/cond/branch_1_fun/all_to_all | solution.py:629
  58.9 12.4 %pair_grams.1 = (f32[2,768,768]{2,1,0:T(8,128)}, f32[2,768,768]{2,1,0:T(8,128)}) custom-call(s32[384]{0:T(512)S(1)} %copy-done.8, bf16[768,1024]{1,0:T(8,128)(2,1)} %get-tuple-element.45.wide_ref, bf16[768,768]{1,0:T(8,128)(2,1)} %get-tuple-element.46.halves_ref, f32[2,768,768]{2,1,0:T(8,128)} %bitcast.25, f32[2,768,768]{2,1,0:T(8,128)} %bitcast.27), custom_call_target="tpu_custom_call" | custom-call | flops 8999999488 | bytes 25000000 | tf_op jit(solution)/shard_map/cond/branch_1_fun/pair_grams/pallas_call | solution.py:722
  71.3 15.3 %all-to-all-done.3.back_ref = bf16[128,56,128]{2,1,0:T(8,128)(2,1)S(1)} async-done(((bf16[128,56,128]{2,1,0:T(8,128)(2,1)}), bf16[128,56,128]{2,1,0:T(8,128)(2,1)S(1)}, u32[]{:S(2)}, u32[]{:S(2)}) %all-to-all-start.3) | async-done | bytes 1835040 | tf_op jit(solution)/shard_map/cond/branch_1_fun/all_to_all | solution.py:629
  86.6 2.6 %unpack_pairs.1 = bf16[16,48,8,96]{3,2,1,0:T(8,128)(2,1)} custom-call(s32[128]{0:T(128)} %get-tuple-element.34.owner_hbm, s32[384]{0:T(512)} %get-tuple-element.35.table_ref.table_hbm, bf16[128,56,128]{2,1,0:T(8,128)(2,1)S(1)} %all-to-all-done.3.back_ref), custom_call_target="tpu_custom_call" | custom-call | tf_op jit(solution)/shard_map/cond/branch_1_fun/unpack_pairs/pallas_call | solution.py:739
Async XLA Ops:
  5.3 12.1 %copy-start.8 = (s32[384]{0:T(512)S(1)}, s32[384]{0:T(512)}, u32[]{:S(2)}) copy-start(s32[384]{0:T(512)} %get-tuple-element.35.table_ref.table_hbm) | copy-start | bytes 4612 | tf_op jit(solution)/shard_map/cond
  5.4 12.1 %collective-permute-start = (bf16[2,768,768]{2,1,0:T(8,128)(2,1)}, bf16[2,768,768]{2,1,0:T(8,128)(2,1)}, u32[]{:S(2)}, u32[]{:S(2)}) collective-permute-start(bf16[2,768,768]{2,1,0:T(8,128)(2,1)} %bitcast.29), channel_id=1, source_target_pairs={{0,1},{1,0},{2,3},{3,2},{4,5},{5,4},{6,7},{7,6},{8,9},{9,8},{10,11... | collective-permute-start | bytes 7077896 | tf_op jit(solution)/shard_map/cond/branch_1_fun/ppermute | solution.py:634
  6.9 10.6 %collective-permute-start.1 = (bf16[2,768,768]{2,1,0:T(8,128)(2,1)}, bf16[2,768,768]{2,1,0:T(8,128)(2,1)}, u32[]{:S(2)}, u32[]{:S(2)}) collective-permute-start(bf16[2,768,768]{2,1,0:T(8,128)(2,1)} %bitcast.32), channel_id=1, source_target_pairs={{0,1},{1,0},{2,3},{3,2},{4,5},{5,4},{6,7},{7,6},{8,9},{9,8},{10,11... | collective-permute-start | bytes 7077896 | tf_op jit(solution)/shard_map/cond/branch_1_fun/ppermute | solution.py:634
  7.0 38.2 %all-to-all-start.2 = ((bf16[128,56,128]{2,1,0:T(8,128)(2,1)}), bf16[128,56,128]{2,1,0:T(8,128)(2,1)S(1)}, u32[]{:S(2)}, u32[]{:S(2)}) async-start(bf16[128,56,128]{2,1,0:T(8,128)(2,1)} %get-tuple-element.36), calls=%async_computation.2 | async-start | bytes 3670016 | tf_op jit(solution)/shard_map/cond/branch_1_fun/all_to_all | solution.py:629
  26.2 20.6 %copy-start.3 = (bf16[768,768]{1,0:T(8,128)(2,1)S(1)}, bf16[768,768]{1,0:T(8,128)(2,1)}, u32[]{:S(2)}) copy-start(bf16[768,768]{1,0:T(8,128)(2,1)} %get-tuple-element.39.left_ref) | copy-start | bytes 3538948 | tf_op jit(solution)/shard_map/cond
  45.8 2.8 %collective-permute-start.2 = (bf16[768,384]{1,0:T(8,128)(2,1)S(1)}, bf16[768,384]{1,0:T(8,128)(2,1)S(1)}, u32[]{:S(2)}, u32[]{:S(2)}) collective-permute-start(bf16[768,384]{1,0:T(8,128)(2,1)S(1)} %extract_extra.1.mine_ref), channel_id=1, source_target_pairs={{0,1},{1,0},{2,3},{3,2},{4,5},{5,4},{6,7},{7,6},{8,9},{9,8},{10,11... | collective-permute-start | bytes 1769480 | tf_op jit(solution)/shard_map/cond/branch_1_fun/ppermute | solution.py:634
  46.8 1.8 %copy-start.6 = (bf16[1024,1024]{1,0:T(8,128)(2,1)S(1)}, bf16[1024,1024]{1,0:T(8,128)(2,1)}, u32[]{:S(2)}) copy-start(bf16[1024,1024]{1,0:T(8,128)(2,1)} %get-tuple-element.41.right0_ref) | copy-start | bytes 6291460 | tf_op jit(solution)/shard_map/cond
  55.1 31.5 %all-to-all-start.3 = ((bf16[128,56,128]{2,1,0:T(8,128)(2,1)}), bf16[128,56,128]{2,1,0:T(8,128)(2,1)S(1)}, u32[]{:S(2)}, u32[]{:S(2)}) async-start(bf16[128,56,128]{2,1,0:T(8,128)(2,1)} %bitcast.23), calls=%async_computation.3 | async-start | bytes 3670016 | tf_op jit(solution)/shard_map/cond/branch_1_fun/all_to_all | solution.py:629

commit v3 on v2

--- a/solution.py
+++ b/solution.py
@@ -439,9 +439,11 @@
     sems,
 ):
     width = root_ref.shape[0]
-    groups = padded_ref.shape[0] // LANES
+    wide_all = padded_ref.shape[1]
+    groups = wide_all // LANES
     part = width // groups
     half = width // 2
+    free = LANES - part
     core = lax.axis_index("mp") % 2
     info_at = table_ref.shape[0] - LANES
     left0_copy = copy_in(left_hbm.at[0], left0_ref, sems.at[0])
@@ -479,6 +481,10 @@
                 rows[:, h * narrow : (h + 1) * narrow], spread, (((1,), (1,)), ((), ())), preferred_element_type=F32
             )
             padded_ref[g * wide : (g + 1) * wide, h * wide : (h + 1) * wide] = cell.astype(BF16)
+    row = lax.broadcasted_iota(jnp.int32, (free * groups, wide_all), 0)
+    col = lax.broadcasted_iota(jnp.int32, (free * groups, wide_all), 1)
+    hit = (col // LANES == row // free) & (col % LANES == part + row % free)
+    padded_ref[wide_all:, :] = jnp.where(hit, 1.0, 0.0).astype(BF16)
     left0_copy.wait()
 
 
@@ -523,8 +529,7 @@
 
 
 def products_kernel(
-    half_ref, right0_ref, mine_ref, other_ref, left1_hbm, right1_hbm, out_hbm, block_hbm, block_ref, left1_ref, right1_ref, top_ref,
-    message_ref, store_sems, sems,
+    half_ref, right0_ref, mine_ref, other_ref, left1_ref, right1_ref, out_hbm, block_hbm, block_ref, message_ref, store_sems, block_sem,
 ):
     row_groups, col_groups, height, _ = message_ref.shape
     row_part = height - 8
@@ -532,8 +537,6 @@
     half = width // 2
     groups = row_part // 8
     core = lax.axis_index("mp") % 2
-    left1_copy = copy_in(left1_hbm, left1_ref, sems.at[0])
-    right1_copy = copy_in(right1_hbm, right1_ref, sems.at[1])
     for j in range(2):
 
         @pl.when(core == j)
@@ -541,35 +544,22 @@
             block_ref[:, j * half : (j + 1) * half] = mine_ref[...]
             block_ref[:, (1 - j) * half : (2 - j) * half] = other_ref[...]
 
-    block_copy = copy_in(block_ref, block_hbm, sems.at[2])
-    take = take_matrix(width // col_groups)
-    wide = take.shape[0]
-    transposed = (((1,), (1,)), ((), ()))
+    block_copy = copy_in(block_ref, block_hbm, block_sem)
     stores = []
     start = 0
     for i, span in enumerate(SPANS):
         rows = slice(start * row_part, (start + span) * row_part)
-        first = jnp.dot(half_ref[rows, :], right0_ref[...], preferred_element_type=F32).astype(BF16)
-        for k in range(span):
-            for m in range(col_groups):
-                message_ref[start + k, m, :row_part] = first[k * row_part : (k + 1) * row_part, m * LANES : (m + 1) * LANES]
-        if i == 0:
-            left1_copy.wait()
-            right1_copy.wait()
         temp = jnp.dot(left1_ref[rows, :], block_ref[...], preferred_element_type=F32).astype(BF16)
         extra = jnp.dot(temp, right1_ref[...], preferred_element_type=F32)
-        top = extra[:, : half - LANES].astype(BF16)
-        for g in range(col_groups * LANES // wide):
-            spread = lax.dot_general(top[:, g * LANES : (g + 1) * LANES], take, transposed, preferred_element_type=F32)
-            top_ref[: span * row_part, g * wide : (g + 1) * wide] = spread.astype(BF16)
+        both = jnp.concatenate([half_ref[rows, :], extra[:, : half - LANES].astype(BF16)], axis=1)
+        result = jnp.dot(both, right0_ref[...], preferred_element_type=F32).astype(BF16)
         low = extra[:, half - LANES :].reshape(span, groups, 8, LANES)
         low = [low[:, k].reshape(8 * span, LANES) for k in range(groups)]
         low += [jnp.zeros((8 * span, LANES), F32)] * (col_groups - groups)
         low = swap_groups(low, LANES // col_groups)
         for k in range(span):
             for m in range(col_groups):
-                cols = slice(m * LANES, (m + 1) * LANES)
-                message_ref[start + k, m, :row_part] += top_ref[k * row_part : (k + 1) * row_part, cols]
+                message_ref[start + k, m, :row_part] = result[k * row_part : (k + 1) * row_part, m * LANES : (m + 1) * LANES]
                 message_ref[start + k, m, row_part:] = low[m][8 * k : 8 * k + 8].astype(BF16)
         part = pl.ds(start, span)
         stores.append(copy_in(message_ref.at[part], out_hbm.at[part], store_sems.at[i]))
@@ -647,6 +637,7 @@
     smem = pl.BlockSpec(memory_space=pltpu.SMEM)
     vmem = pl.BlockSpec(memory_space=pltpu.VMEM)
     hbm = pl.BlockSpec(memory_space=HBM)
+    anywhere = pl.BlockSpec(memory_space=pl.ANY)
     dma = pltpu.SemaphoreType.DMA
     message_shape = (dp_count, mp_count, height, LANES)
     left_root = left_root[0, 0]
@@ -665,7 +656,7 @@
     padded, picked, left0, left1 = pl.pallas_call(
         prepare_kernel,
         out_shape=[
-            HBM((wide, wide), BF16),
+            HBM((wide + mp_count * (LANES - col_part), wide), BF16),
             HBM((width, width // 2), BF16),
             HBM((width, width), BF16),
             HBM((width, width), BF16),
@@ -701,21 +692,18 @@
     leaving, halves = pl.pallas_call(
         products_kernel,
         out_shape=[HBM(message_shape, BF16), HBM((width, width), BF16)],
-        in_specs=[vmem] * 4 + [hbm] * 2,
+        in_specs=[vmem] * 6,
         out_specs=[hbm] * 2,
         scratch_shapes=[
             pltpu.VMEM((width, width), BF16),
-            pltpu.VMEM((width, width), BF16),
-            pltpu.VMEM((width, width // 2), BF16),
-            pltpu.VMEM((max(SPANS) * row_part, wide), BF16),
             pltpu.VMEM(message_shape, BF16),
             dma((len(SPANS),)),
-            dma((3,)),
+            dma,
         ],
         cost_estimate=cost(5, 12),
         compiler_params=params(28),
         name="precondition",
-    )(half, padded, mine, other, in_hbm(left1), in_hbm(picked))
+    )(half, padded, mine, other, left1, picked)
     returned = exchange(leaving.reshape(outgoing.shape))
     tile = width // 3
     stat_spec = pl.BlockSpec((1, tile, width), lambda s, i: (s, i, 0))
@@ -739,7 +727,7 @@
     precond = pl.pallas_call(
         unpack_pairs_kernel,
         out_shape=HBM(gradient.shape, BF16),
-        in_specs=[hbm, hbm, vmem],
+        in_specs=[anywhere, anywhere, vmem],
         out_specs=hbm,
         scratch_shapes=[
             pltpu.SMEM(owner.shape, jnp.int32),
@@ -751,7 +739,7 @@
         ],
         compiler_params=params(12),
         name="unpack_pairs",
-    )(in_hbm(owner), in_hbm(table), returned)
+    )(owner, table, returned)
     return (precond, left_new[None, None], right_new[None, None])
 
 

time: 90.1 us -> 89.4 us (level)
  Pallas kernels: 36.6 us -> 35.4 us
  local copies, waits for them, and re-layouts: 0.01 us -> 1 us
    pallas_call x1, Pallas kernels: 6.5 us -> 5.23 us  [pair_path(): pl.pallas_call(products_kernel, out_shape=[HBM(message_shape, BF16), HBM(...]
    cond x6 -> x12, local copies, waits for them, and re-layouts: 0.01 us -> 1 us
where the time goes in v3:
time: 89.4 us; the launch traced here: 89 us
  Pallas kernels  35.4 us (40%)
  waiting for transfers between devices  33.8 us (38%)
  starting transfers between devices  16.9 us (19%)
  between operations  1.49 us (2%)
  local copies, waits for them, and re-layouts  1 us (1%)
    all_to_all x2, waiting for transfers between devices, exchange(): lax.all_to_all(x, ('dp', 'mp'), split_axis=0, concat_axis=0, tiled=True)  33.8 us
    all_to_all x2, starting transfers between devices, exchange(): lax.all_to_all(x, ('dp', 'mp'), split_axis=0, concat_axis=0, tiled=True)  14.3 us
    pallas_call x1, Pallas kernels, pair_path(): pl.pallas_call(pair_gram_kernel, grid=(slots, width // tile), out_shape=[...  12.4 us
    pallas_call x1, Pallas kernels, pair_path(): pl.pallas_call(prepare_kernel, out_shape=[HBM((wide + mp_count * (LANES -...  8.96 us
    pallas_call x1, Pallas kernels, pair_path(): pl.pallas_call(products_kernel, out_shape=[HBM(message_shape, BF16), HBM(...  5.23 us
    pallas_call x1, Pallas kernels, per_device(): pl.pallas_call(pack_pairs_kernel, out_shape=[HBM((devices, height, LANES)...  4.02 us
    ppermute x3, starting transfers between devices, other_core(): return lax.ppermute(x, 'mp', [(i, i ^ 1) for i in range(count)])  2.58 us
    pallas_call x1, Pallas kernels, pair_path(): pl.pallas_call(unpack_pairs_kernel, out_shape=HBM(gradient.shape, BF16),...  2.45 us
  transfers between devices with their start and end apart: 5, of which 2 were waited for; matrix products, arithmetic and copies ran while one was open for 0% of the time, Pallas kernels for 26%

profile of v3, /device:TPU:1, one launch (start us, length us, event | category | flops | bytes accessed | tf_op | source)
XLA Modules:
  0.0 89.0 jit_solution(5342074918282456971)
XLA Ops:
  0.6 4.0 %pack_pairs.1 = (bf16[128,56,128]{2,1,0:T(8,128)(2,1)}, s32[384]{0:T(512)}, s32[128]{0:T(128)}) custom-call(s32[128]{0:T(128)} %owner_hbm.1, bf16[16,48,8,96]{3,2,1,0:T(8,128)(2,1)} %grad_hbm.1), custom_call_target="tpu_custom_call" | custom-call | tf_op jit(solution)/shard_map/pack_pairs/pallas_call | solution.py:752
  5.3 83.5 %conditional.1 = (bf16[16,48,8,96]{3,2,1,0:T(8,128)(2,1)}, f32[1,1,2,768,768]{4,3,2,1,0:T(8,128)}, f32[1,1,2,768,768]{4,3,2,1,0:T(8,128)}) conditional(s32[]{:T(128)} %bitcast.16, (s32[128]{0:T(128)}, bf16[16,48,8,96]{3,2,1,0:T(8,128)(2,1)}, bf16[1,1,2,768,768]{4,3,2,1,0:T(8,128)(2,1)}, bf16[1,1,2,768,768]{4,3,2,1,0:T(8,128)(2,1)}, ...), branch_computations={%region_0.0_spmd, %region_1.0_spmd} | conditional | flops 22599999488 | bytes 132179840 | solution.py:781
  5.3 0.0 copy-start.11
  5.3 1.5 %collective-permute-start = (bf16[2,768,768]{2,1,0:T(8,128)(2,1)}, bf16[2,768,768]{2,1,0:T(8,128)(2,1)}, u32[]{:S(2)}, u32[]{:S(2)}) collective-permute-start(bf16[2,768,768]{2,1,0:T(8,128)(2,1)} %bitcast.29), channel_id=1, source_target_pairs={{0,1},{1,0},{2,3},{3,2},{4,5},{5,4},{6,7},{7,6},{8,9},{9,8},{10,11... | collective-permute-start | bytes 7077896 | tf_op jit(solution)/shard_map/cond/branch_1_fun/ppermute | solution.py:624
  6.8 0.1 collective-permute-start.1
  6.9 10.5 %all-to-all-start.2 = ((bf16[128,56,128]{2,1,0:T(8,128)(2,1)}), bf16[128,56,128]{2,1,0:T(8,128)(2,1)S(1)}, u32[]{:S(2)}, u32[]{:S(2)}) async-start(bf16[128,56,128]{2,1,0:T(8,128)(2,1)} %get-tuple-element.36), calls=%async_computation.2 | async-start | bytes 3670016 | tf_op jit(solution)/shard_map/cond/branch_1_fun/all_to_all | solution.py:619
  17.4 0.0 collective-permute-done.left_other_hbm
  17.5 0.0 collective-permute-done.1.right_other_hbm
  17.5 0.0 copy-done.11
  17.5 9.0 %prepare_roots.1 = (bf16[1280,1024]{1,0:T(8,128)(2,1)}, bf16[768,384]{1,0:T(8,128)(2,1)}, bf16[768,768]{1,0:T(8,128)(2,1)}, bf16[768,768]{1,0:T(8,128)(2,1)}) custom-call(s32[384]{0:T(512)S(1)} %copy-done.11, bf16[2,768,768]{2,1,0:T(8,128)(2,1)} %bitcast.30, bf16[2,768,768]{2,1,0:T(8,128)(2,1)} %bitcast.33, ...), custom_call_target="tpu_custom_call" | custom-call | flops 6000000000 | bytes 9000000 | tf_op jit(solution)/shard_map/cond/branch_1_fun/prepare_roots/pallas_call | solution.py:656
  26.4 0.0 copy-start.4
  26.5 18.7 %all-to-all-done.2 = bf16[128,56,128]{2,1,0:T(8,128)(2,1)S(1)} async-done(((bf16[128,56,128]{2,1,0:T(8,128)(2,1)}), bf16[128,56,128]{2,1,0:T(8,128)(2,1)S(1)}, u32[]{:S(2)}, u32[]{:S(2)}) %all-to-all-start.2) | async-done | bytes 1835040 | tf_op jit(solution)/shard_map/cond/branch_1_fun/all_to_all | solution.py:619
  45.1 0.6 extract_extra.1.mine_ref
  45.8 1.0 %collective-permute-start.2 = (bf16[768,384]{1,0:T(8,128)(2,1)S(1)}, bf16[768,384]{1,0:T(8,128)(2,1)S(1)}, u32[]{:S(2)}, u32[]{:S(2)}) collective-permute-start(bf16[768,384]{1,0:T(8,128)(2,1)S(1)} %extract_extra.1.mine_ref), channel_id=1, source_target_pairs={{0,1},{1,0},{2,3},{3,2},{4,5},{5,4},{6,7},{7,6},{8,9},{9,8},{10,11... | collective-permute-start | bytes 1769480 | tf_op jit(solution)/shard_map/cond/branch_1_fun/ppermute | solution.py:624
  46.7 0.0 copy-done.4
  46.7 0.0 copy-start.3
  46.7 0.0 copy-start.7
  46.7 0.0 copy-start.8
  46.7 1.8 %half_product.1 = (bf16[768,1024]{1,0:T(8,128)(2,1)S(1)}, bf16[768,1024]{1,0:T(8,128)(2,1)}) custom-call(bf16[16,8,56,128]{3,2,1,0:T(8,128)(2,1)S(1)} %bitcast.19, bf16[768,768]{1,0:T(8,128)(2,1)S(1)} %copy-done.4), custom_call_target="tpu_custom_call" | custom-call | flops 2000000000 | bytes 6000000 | tf_op jit(solution)/shard_map/cond/branch_1_fun/half_product/pallas_call | solution.py:682
  48.5 0.0 collective-permute-done.2.other_ref
  48.5 0.0 copy-done.3
  48.5 0.9 copy-done.7
  49.4 0.1 copy-done.8
  49.5 5.2 %precondition.3 = (bf16[16,8,56,128]{3,2,1,0:T(8,128)(2,1)}, bf16[768,768]{1,0:T(8,128)(2,1)}) custom-call(bf16[768,1024]{1,0:T(8,128)(2,1)S(1)} %get-tuple-element.40.half_ref, bf16[1280,1024]{1,0:T(8,128)(2,1)S(1)} %copy-done.7, bf16[768,384]{1,0:T(8,128)(2,1)S(1)} %extract_extra.1.mine_ref, bf16[768,384]{1,0:T(8,128)(2,1)S(1)} %collective-permute-done.2.other_ref, ...), custom_call_target="tpu_custom_call" | custom-call | flops 5000000000 | bytes 12000000 | tf_op jit(solution)/shard_map/cond/branch_1_fun/precondition/pallas_call | solution.py:692
  54.7 3.8 %all-to-all-start.3 = ((bf16[128,56,128]{2,1,0:T(8,128)(2,1)}), bf16[128,56,128]{2,1,0:T(8,128)(2,1)S(1)}, u32[]{:S(2)}, u32[]{:S(2)}) async-start(bf16[128,56,128]{2,1,0:T(8,128)(2,1)} %bitcast.23), calls=%async_computation.3 | async-start | bytes 3670016 | tf_op jit(solution)/shard_map/cond/branch_1_fun/all_to_all | solution.py:619
  58.6 0.0 copy-start.10
  58.6 12.4 %pair_grams.1 = (f32[2,768,768]{2,1,0:T(8,128)}, f32[2,768,768]{2,1,0:T(8,128)}) custom-call(s32[384]{0:T(512)S(1)} %copy-done.11, bf16[768,1024]{1,0:T(8,128)(2,1)} %get-tuple-element.45.wide_ref, bf16[768,768]{1,0:T(8,128)(2,1)} %get-tuple-element.46.halves_ref, f32[2,768,768]{2,1,0:T(8,128)} %bitcast.25, f32[2,768,768]{2,1,0:T(8,128)} %bitcast.27), custom_call_target="tpu_custom_call" | custom-call | flops 8999999488 | bytes 25000000 | tf_op jit(solution)/shard_map/cond/branch_1_fun/pair_grams/pallas_call | solution.py:710
  71.0 15.1 %all-to-all-done.3.back_ref = bf16[128,56,128]{2,1,0:T(8,128)(2,1)S(1)} async-done(((bf16[128,56,128]{2,1,0:T(8,128)(2,1)}), bf16[128,56,128]{2,1,0:T(8,128)(2,1)S(1)}, u32[]{:S(2)}, u32[]{:S(2)}) %all-to-all-start.3) | async-done | bytes 1835040 | tf_op jit(solution)/shard_map/cond/branch_1_fun/all_to_all | solution.py:619
  86.1 0.0 copy-done.10
  86.1 2.4 %unpack_pairs.1 = bf16[16,48,8,96]{3,2,1,0:T(8,128)(2,1)} custom-call(s32[128]{0:T(128)S(1)} %copy-done.10, s32[384]{0:T(512)S(1)} %copy-done.11, bf16[128,56,128]{2,1,0:T(8,128)(2,1)S(1)} %all-to-all-done.3.back_ref), custom_call_target="tpu_custom_call" | custom-call | tf_op jit(solution)/shard_map/cond/branch_1_fun/unpack_pairs/pallas_call | solution.py:727
Async XLA Ops:
  5.3 12.1 %copy-start.11 = (s32[384]{0:T(512)S(1)}, s32[384]{0:T(512)}, u32[]{:S(2)}) copy-start(s32[384]{0:T(512)} %get-tuple-element.35.table_ref.table_hbm) | copy-start | bytes 4612 | tf_op jit(solution)/shard_map/cond
  5.3 12.1 %collective-permute-start = (bf16[2,768,768]{2,1,0:T(8,128)(2,1)}, bf16[2,768,768]{2,1,0:T(8,128)(2,1)}, u32[]{:S(2)}, u32[]{:S(2)}) collective-permute-start(bf16[2,768,768]{2,1,0:T(8,128)(2,1)} %bitcast.29), channel_id=1, source_target_pairs={{0,1},{1,0},{2,3},{3,2},{4,5},{5,4},{6,7},{7,6},{8,9},{9,8},{10,11... | collective-permute-start | bytes 7077896 | tf_op jit(solution)/shard_map/cond/branch_1_fun/ppermute | solution.py:624
  6.8 10.6 %collective-permute-start.1 = (bf16[2,768,768]{2,1,0:T(8,128)(2,1)}, bf16[2,768,768]{2,1,0:T(8,128)(2,1)}, u32[]{:S(2)}, u32[]{:S(2)}) collective-permute-start(bf16[2,768,768]{2,1,0:T(8,128)(2,1)} %bitcast.32), channel_id=1, source_target_pairs={{0,1},{1,0},{2,3},{3,2},{4,5},{5,4},{6,7},{7,6},{8,9},{9,8},{10,11... | collective-permute-start | bytes 7077896 | tf_op jit(solution)/shard_map/cond/branch_1_fun/ppermute | solution.py:624
  6.9 38.2 %all-to-all-start.2 = ((bf16[128,56,128]{2,1,0:T(8,128)(2,1)}), bf16[128,56,128]{2,1,0:T(8,128)(2,1)S(1)}, u32[]{:S(2)}, u32[]{:S(2)}) async-start(bf16[128,56,128]{2,1,0:T(8,128)(2,1)} %get-tuple-element.36), calls=%async_computation.2 | async-start | bytes 3670016 | tf_op jit(solution)/shard_map/cond/branch_1_fun/all_to_all | solution.py:619
  26.4 20.3 %copy-start.4 = (bf16[768,768]{1,0:T(8,128)(2,1)S(1)}, bf16[768,768]{1,0:T(8,128)(2,1)}, u32[]{:S(2)}) copy-start(bf16[768,768]{1,0:T(8,128)(2,1)} %get-tuple-element.39.left_ref) | copy-start | bytes 3538948 | tf_op jit(solution)/shard_map/cond
  45.8 2.8 %collective-permute-start.2 = (bf16[768,384]{1,0:T(8,128)(2,1)S(1)}, bf16[768,384]{1,0:T(8,128)(2,1)S(1)}, u32[]{:S(2)}, u32[]{:S(2)}) collective-permute-start(bf16[768,384]{1,0:T(8,128)(2,1)S(1)} %extract_extra.1.mine_ref), channel_id=1, source_target_pairs={{0,1},{1,0},{2,3},{3,2},{4,5},{5,4},{6,7},{7,6},{8,9},{9,8},{10,11... | collective-permute-start | bytes 1769480 | tf_op jit(solution)/shard_map/cond/branch_1_fun/ppermute | solution.py:624
  46.7 1.8 %copy-start.3 = (bf16[768,768]{1,0:T(8,128)(2,1)S(1)}, bf16[768,768]{1,0:T(8,128)(2,1)}, u32[]{:S(2)}) copy-start(bf16[768,768]{1,0:T(8,128)(2,1)} %get-tuple-element.42.roots_hbm.left1_ref) | copy-start | bytes 3538948 | tf_op jit(solution)/shard_map/cond
  46.7 2.7 %copy-start.7 = (bf16[1280,1024]{1,0:T(8,128)(2,1)S(1)}, bf16[1280,1024]{1,0:T(8,128)(2,1)}, u32[]{:S(2)}) copy-start(bf16[1280,1024]{1,0:T(8,128)(2,1)} %get-tuple-element.41.right0_ref) | copy-start | bytes 7864324 | tf_op jit(solution)/shard_map/cond
  46.7 2.8 %copy-start.8 = (bf16[768,384]{1,0:T(8,128)(2,1)S(1)}, bf16[768,384]{1,0:T(8,128)(2,1)}, u32[]{:S(2)}) copy-start(bf16[768,384]{1,0:T(8,128)(2,1)} %get-tuple-element.43.right1_ref) | copy-start | bytes 1769476 | tf_op jit(solution)/shard_map/cond
  54.7 31.3 %all-to-all-start.3 = ((bf16[128,56,128]{2,1,0:T(8,128)(2,1)}), bf16[128,56,128]{2,1,0:T(8,128)(2,1)S(1)}, u32[]{:S(2)}, u32[]{:S(2)}) async-start(bf16[128,56,128]{2,1,0:T(8,128)(2,1)} %bitcast.23), calls=%async_computation.3 | async-start | bytes 3670016 | tf_op jit(solution)/shard_map/cond/branch_1_fun/all_to_all | solution.py:619
  58.6 27.5 %copy-start.10 = (s32[128]{0:T(128)S(1)}, s32[128]{0:T(128)}, u32[]{:S(2)}) copy-start(s32[128]{0:T(128)} %get-tuple-element.34.owner_hbm) | copy-start | bytes 1540 | tf_op jit(solution)/shard_map/cond

commit v4 on v3

--- a/solution.py
+++ b/solution.py
@@ -306,13 +306,17 @@
         out_ref[d] = jnp.concatenate([tile, jnp.zeros((height - row_part, LANES), F32)], axis=0).astype(BF16)
         return carry
 
-    stores = []
     pieces = store_sems.shape[0]
     share = devices // pieces
-    for i in range(pieces):
-        lax.fori_loop(i * share, (i + 1) * share, message, 0, unroll=8)
-
-        def extra(e, carry, i=i):
+
+    def store(i):
+        part = pl.ds(i * share, share)
+        return pltpu.make_async_copy(out_ref.at[part], out_hbm.at[part], store_sems.at[i])
+
+    def piece(i, carry):
+        lax.fori_loop(0, share, lambda d, carry: message(i * share + d, carry), 0, unroll=8)
+
+        def extra(e, carry):
             block = table_ref[extras_at + e]
             chip = owner_ref[block] // 2
 
@@ -334,12 +338,14 @@
             return carry
 
         lax.fori_loop(0, extras, extra, 0)
-        part = pl.ds(i * share, share)
-        stores.append(copy_in(out_ref.at[part], out_hbm.at[part], store_sems.at[i]))
+        store(i).start()
+        return carry
+
+    lax.fori_loop(0, pieces, piece, 0)
     table_copy.wait()
     bad_copy.wait()
-    for store in stores:
-        store.wait()
+    for i in range(pieces):
+        store(i).wait()
 
 
 def unpack_pairs_kernel(owner_hbm, table_hbm, back_ref, out_hbm, owner_ref, table_ref, out_ref, rows_ref, sems, store_sems):
@@ -371,11 +377,14 @@
         block_row(2 * t + 1, 1)
         return carry
 
-    stores = []
-    for i in range(chunks):
-        lax.fori_loop(i * span // 2, (i + 1) * span // 2, body, 0)
-
-        def extra(e, carry, i=i):
+    def store(i):
+        part = pl.ds(i * span, span)
+        return pltpu.make_async_copy(out_ref.at[part], out_hbm.at[part], store_sems.at[i])
+
+    def piece(i, carry):
+        lax.fori_loop(0, span // 2, lambda t, carry: body(i * (span // 2) + t, carry), 0)
+
+        def extra(e, carry):
             block = table_ref[devices + e]
             chip = owner_ref[block] // 2
             r = block // col_blocks
@@ -401,10 +410,12 @@
             return carry
 
         lax.fori_loop(0, table_ref[2 * devices + 3], extra, 0)
-        part = pl.ds(i * span, span)
-        stores.append(copy_in(out_ref.at[part], out_hbm.at[part], store_sems.at[i]))
-    for store in stores:
-        store.wait()
+        store(i).start()
+        return carry
+
+    lax.fori_loop(0, chunks, piece, 0)
+    for i in range(chunks):
+        store(i).wait()
 
 
 def halves_order(shape, core, axis, part, groups):

time: 89.4 us -> 89.5 us (level)
  no operation moved by 1% of the time
where the time goes in v4:
time: 89.5 us; the launch traced here: 89.1 us
  Pallas kernels  35.5 us (40%)
  waiting for transfers between devices  33.8 us (38%)
  starting transfers between devices  16.9 us (19%)
  between operations  1.49 us (2%)
  local copies, waits for them, and re-layouts  1 us (1%)
    all_to_all x2, waiting for transfers between devices, exchange(): lax.all_to_all(x, ('dp', 'mp'), split_axis=0, concat_axis=0, tiled=True)  33.8 us
    all_to_all x2, starting transfers between devices, exchange(): lax.all_to_all(x, ('dp', 'mp'), split_axis=0, concat_axis=0, tiled=True)  14.3 us
    pallas_call x1, Pallas kernels, pair_path(): pl.pallas_call(pair_gram_kernel, grid=(slots, width // tile), out_shape=[...  12.4 us
    pallas_call x1, Pallas kernels, pair_path(): pl.pallas_call(prepare_kernel, out_shape=[HBM((wide + mp_count * (LANES -...  8.95 us
    pallas_call x1, Pallas kernels, pair_path(): pl.pallas_call(products_kernel, out_shape=[HBM(message_shape, BF16), HBM(...  5.23 us
    pallas_call x1, Pallas kernels, per_device(): pl.pallas_call(pack_pairs_kernel, out_shape=[HBM((devices, height, LANES)...  4.09 us
    ppermute x3, starting transfers between devices, other_core(): return lax.ppermute(x, 'mp', [(i, i ^ 1) for i in range(count)])  2.57 us
    pallas_call x1, Pallas kernels, pair_path(): pl.pallas_call(unpack_pairs_kernel, out_shape=HBM(gradient.shape, BF16),...  2.47 us
  transfers between devices with their start and end apart: 5, of which 2 were waited for; matrix products, arithmetic and copies ran while one was open for 0% of the time, Pallas kernels for 26%

profile of v4, /device:TPU:1, one launch (start us, length us, event | category | flops | bytes accessed | tf_op | source)
XLA Modules:
  0.0 89.1 jit_solution(18331023436954332723)
XLA Ops:
  0.6 4.1 %pack_pairs.1 = (bf16[128,56,128]{2,1,0:T(8,128)(2,1)}, s32[384]{0:T(512)}, s32[128]{0:T(128)}) custom-call(s32[128]{0:T(128)} %owner_hbm.1, bf16[16,48,8,96]{3,2,1,0:T(8,128)(2,1)} %grad_hbm.1), custom_call_target="tpu_custom_call" | custom-call | tf_op jit(solution)/shard_map/pack_pairs/pallas_call | solution.py:763
  5.4 83.5 %conditional.1 = (bf16[16,48,8,96]{3,2,1,0:T(8,128)(2,1)}, f32[1,1,2,768,768]{4,3,2,1,0:T(8,128)}, f32[1,1,2,768,768]{4,3,2,1,0:T(8,128)}) conditional(s32[]{:T(128)} %bitcast.16, (s32[128]{0:T(128)}, bf16[16,48,8,96]{3,2,1,0:T(8,128)(2,1)}, bf16[1,1,2,768,768]{4,3,2,1,0:T(8,128)(2,1)}, bf16[1,1,2,768,768]{4,3,2,1,0:T(8,128)(2,1)}, ...), branch_computations={%region_0.0_spmd, %region_1.0_spmd} | conditional | flops 22599999488 | bytes 132179840 | solution.py:792
  5.4 0.0 copy-start.11
  5.4 1.5 %collective-permute-start = (bf16[2,768,768]{2,1,0:T(8,128)(2,1)}, bf16[2,768,768]{2,1,0:T(8,128)(2,1)}, u32[]{:S(2)}, u32[]{:S(2)}) collective-permute-start(bf16[2,768,768]{2,1,0:T(8,128)(2,1)} %bitcast.29), channel_id=1, source_target_pairs={{0,1},{1,0},{2,3},{3,2},{4,5},{5,4},{6,7},{7,6},{8,9},{9,8},{10,11... | collective-permute-start | bytes 7077896 | tf_op jit(solution)/shard_map/cond/branch_1_fun/ppermute | solution.py:635
  6.9 0.1 collective-permute-start.1
  7.0 10.5 %all-to-all-start.2 = ((bf16[128,56,128]{2,1,0:T(8,128)(2,1)}), bf16[128,56,128]{2,1,0:T(8,128)(2,1)S(1)}, u32[]{:S(2)}, u32[]{:S(2)}) async-start(bf16[128,56,128]{2,1,0:T(8,128)(2,1)} %get-tuple-element.36), calls=%async_computation.2 | async-start | bytes 3670016 | tf_op jit(solution)/shard_map/cond/branch_1_fun/all_to_all | solution.py:630
  17.5 0.0 collective-permute-done.left_other_hbm
  17.5 0.0 collective-permute-done.1.right_other_hbm
  17.5 0.0 copy-done.11
  17.5 9.0 %prepare_roots.1 = (bf16[1280,1024]{1,0:T(8,128)(2,1)}, bf16[768,384]{1,0:T(8,128)(2,1)}, bf16[768,768]{1,0:T(8,128)(2,1)}, bf16[768,768]{1,0:T(8,128)(2,1)}) custom-call(s32[384]{0:T(512)S(1)} %copy-done.11, bf16[2,768,768]{2,1,0:T(8,128)(2,1)} %bitcast.30, bf16[2,768,768]{2,1,0:T(8,128)(2,1)} %bitcast.33, ...), custom_call_target="tpu_custom_call" | custom-call | flops 6000000000 | bytes 9000000 | tf_op jit(solution)/shard_map/cond/branch_1_fun/prepare_roots/pallas_call | solution.py:667
  26.5 0.0 copy-start.4
  26.5 18.7 %all-to-all-done.2 = bf16[128,56,128]{2,1,0:T(8,128)(2,1)S(1)} async-done(((bf16[128,56,128]{2,1,0:T(8,128)(2,1)}), bf16[128,56,128]{2,1,0:T(8,128)(2,1)S(1)}, u32[]{:S(2)}, u32[]{:S(2)}) %all-to-all-start.2) | async-done | bytes 1835040 | tf_op jit(solution)/shard_map/cond/branch_1_fun/all_to_all | solution.py:630
  45.2 0.6 extract_extra.1.mine_ref
  45.8 1.0 %collective-permute-start.2 = (bf16[768,384]{1,0:T(8,128)(2,1)S(1)}, bf16[768,384]{1,0:T(8,128)(2,1)S(1)}, u32[]{:S(2)}, u32[]{:S(2)}) collective-permute-start(bf16[768,384]{1,0:T(8,128)(2,1)S(1)} %extract_extra.1.mine_ref), channel_id=1, source_target_pairs={{0,1},{1,0},{2,3},{3,2},{4,5},{5,4},{6,7},{7,6},{8,9},{9,8},{10,11... | collective-permute-start | bytes 1769480 | tf_op jit(solution)/shard_map/cond/branch_1_fun/ppermute | solution.py:635
  46.8 0.0 copy-done.4
  46.8 0.0 copy-start.3
  46.8 0.0 copy-start.7
  46.8 0.0 copy-start.8
  46.8 1.8 %half_product.1 = (bf16[768,1024]{1,0:T(8,128)(2,1)S(1)}, bf16[768,1024]{1,0:T(8,128)(2,1)}) custom-call(bf16[16,8,56,128]{3,2,1,0:T(8,128)(2,1)S(1)} %bitcast.19, bf16[768,768]{1,0:T(8,128)(2,1)S(1)} %copy-done.4), custom_call_target="tpu_custom_call" | custom-call | flops 2000000000 | bytes 6000000 | tf_op jit(solution)/shard_map/cond/branch_1_fun/half_product/pallas_call | solution.py:693
  48.6 0.0 collective-permute-done.2.other_ref
  48.6 0.0 copy-done.3
  48.6 0.9 copy-done.7
  49.5 0.1 copy-done.8
  49.6 5.2 %precondition.3 = (bf16[16,8,56,128]{3,2,1,0:T(8,128)(2,1)}, bf16[768,768]{1,0:T(8,128)(2,1)}) custom-call(bf16[768,1024]{1,0:T(8,128)(2,1)S(1)} %get-tuple-element.40.half_ref, bf16[1280,1024]{1,0:T(8,128)(2,1)S(1)} %copy-done.7, bf16[768,384]{1,0:T(8,128)(2,1)S(1)} %extract_extra.1.mine_ref, bf16[768,384]{1,0:T(8,128)(2,1)S(1)} %collective-permute-done.2.other_ref, ...), custom_call_target="tpu_custom_call" | custom-call | flops 5000000000 | bytes 12000000 | tf_op jit(solution)/shard_map/cond/branch_1_fun/precondition/pallas_call | solution.py:703
  54.8 3.8 %all-to-all-start.3 = ((bf16[128,56,128]{2,1,0:T(8,128)(2,1)}), bf16[128,56,128]{2,1,0:T(8,128)(2,1)S(1)}, u32[]{:S(2)}, u32[]{:S(2)}) async-start(bf16[128,56,128]{2,1,0:T(8,128)(2,1)} %bitcast.23), calls=%async_computation.3 | async-start | bytes 3670016 | tf_op jit(solution)/shard_map/cond/branch_1_fun/all_to_all | solution.py:630
  58.6 0.0 copy-start.10
  58.7 12.4 %pair_grams.1 = (f32[2,768,768]{2,1,0:T(8,128)}, f32[2,768,768]{2,1,0:T(8,128)}) custom-call(s32[384]{0:T(512)S(1)} %copy-done.11, bf16[768,1024]{1,0:T(8,128)(2,1)} %get-tuple-element.45.wide_ref, bf16[768,768]{1,0:T(8,128)(2,1)} %get-tuple-element.46.halves_ref, f32[2,768,768]{2,1,0:T(8,128)} %bitcast.25, f32[2,768,768]{2,1,0:T(8,128)} %bitcast.27), custom_call_target="tpu_custom_call" | custom-call | flops 8999999488 | bytes 25000000 | tf_op jit(solution)/shard_map/cond/branch_1_fun/pair_grams/pallas_call | solution.py:721
  71.1 15.1 %all-to-all-done.3.back_ref = bf16[128,56,128]{2,1,0:T(8,128)(2,1)S(1)} async-done(((bf16[128,56,128]{2,1,0:T(8,128)(2,1)}), bf16[128,56,128]{2,1,0:T(8,128)(2,1)S(1)}, u32[]{:S(2)}, u32[]{:S(2)}) %all-to-all-start.3) | async-done | bytes 1835040 | tf_op jit(solution)/shard_map/cond/branch_1_fun/all_to_all | solution.py:630
  86.2 0.0 copy-done.10
  86.2 2.5 %unpack_pairs.1 = bf16[16,48,8,96]{3,2,1,0:T(8,128)(2,1)} custom-call(s32[128]{0:T(128)S(1)} %copy-done.10, s32[384]{0:T(512)S(1)} %copy-done.11, bf16[128,56,128]{2,1,0:T(8,128)(2,1)S(1)} %all-to-all-done.3.back_ref), custom_call_target="tpu_custom_call" | custom-call | tf_op jit(solution)/shard_map/cond/branch_1_fun/unpack_pairs/pallas_call | solution.py:738
Async XLA Ops:
  5.4 12.1 %copy-start.11 = (s32[384]{0:T(512)S(1)}, s32[384]{0:T(512)}, u32[]{:S(2)}) copy-start(s32[384]{0:T(512)} %get-tuple-element.35.table_ref.table_hbm) | copy-start | bytes 4612 | tf_op jit(solution)/shard_map/cond
  5.4 12.1 %collective-permute-start = (bf16[2,768,768]{2,1,0:T(8,128)(2,1)}, bf16[2,768,768]{2,1,0:T(8,128)(2,1)}, u32[]{:S(2)}, u32[]{:S(2)}) collective-permute-start(bf16[2,768,768]{2,1,0:T(8,128)(2,1)} %bitcast.29), channel_id=1, source_target_pairs={{0,1},{1,0},{2,3},{3,2},{4,5},{5,4},{6,7},{7,6},{8,9},{9,8},{10,11... | collective-permute-start | bytes 7077896 | tf_op jit(solution)/shard_map/cond/branch_1_fun/ppermute | solution.py:635
  6.9 10.6 %collective-permute-start.1 = (bf16[2,768,768]{2,1,0:T(8,128)(2,1)}, bf16[2,768,768]{2,1,0:T(8,128)(2,1)}, u32[]{:S(2)}, u32[]{:S(2)}) collective-permute-start(bf16[2,768,768]{2,1,0:T(8,128)(2,1)} %bitcast.32), channel_id=1, source_target_pairs={{0,1},{1,0},{2,3},{3,2},{4,5},{5,4},{6,7},{7,6},{8,9},{9,8},{10,11... | collective-permute-start | bytes 7077896 | tf_op jit(solution)/shard_map/cond/branch_1_fun/ppermute | solution.py:635
  7.0 38.2 %all-to-all-start.2 = ((bf16[128,56,128]{2,1,0:T(8,128)(2,1)}), bf16[128,56,128]{2,1,0:T(8,128)(2,1)S(1)}, u32[]{:S(2)}, u32[]{:S(2)}) async-start(bf16[128,56,128]{2,1,0:T(8,128)(2,1)} %get-tuple-element.36), calls=%async_computation.2 | async-start | bytes 3670016 | tf_op jit(solution)/shard_map/cond/branch_1_fun/all_to_all | solution.py:630
  26.5 20.3 %copy-start.4 = (bf16[768,768]{1,0:T(8,128)(2,1)S(1)}, bf16[768,768]{1,0:T(8,128)(2,1)}, u32[]{:S(2)}) copy-start(bf16[768,768]{1,0:T(8,128)(2,1)} %get-tuple-element.39.left_ref) | copy-start | bytes 3538948 | tf_op jit(solution)/shard_map/cond
  45.8 2.8 %collective-permute-start.2 = (bf16[768,384]{1,0:T(8,128)(2,1)S(1)}, bf16[768,384]{1,0:T(8,128)(2,1)S(1)}, u32[]{:S(2)}, u32[]{:S(2)}) collective-permute-start(bf16[768,384]{1,0:T(8,128)(2,1)S(1)} %extract_extra.1.mine_ref), channel_id=1, source_target_pairs={{0,1},{1,0},{2,3},{3,2},{4,5},{5,4},{6,7},{7,6},{8,9},{9,8},{10,11... | collective-permute-start | bytes 1769480 | tf_op jit(solution)/shard_map/cond/branch_1_fun/ppermute | solution.py:635
  46.8 1.8 %copy-start.3 = (bf16[768,768]{1,0:T(8,128)(2,1)S(1)}, bf16[768,768]{1,0:T(8,128)(2,1)}, u32[]{:S(2)}) copy-start(bf16[768,768]{1,0:T(8,128)(2,1)} %get-tuple-element.42.roots_hbm.left1_ref) | copy-start | bytes 3538948 | tf_op jit(solution)/shard_map/cond
  46.8 2.7 %copy-start.7 = (bf16[1280,1024]{1,0:T(8,128)(2,1)S(1)}, bf16[1280,1024]{1,0:T(8,128)(2,1)}, u32[]{:S(2)}) copy-start(bf16[1280,1024]{1,0:T(8,128)(2,1)} %get-tuple-element.41.right0_ref) | copy-start | bytes 7864324 | tf_op jit(solution)/shard_map/cond
  46.8 2.8 %copy-start.8 = (bf16[768,384]{1,0:T(8,128)(2,1)S(1)}, bf16[768,384]{1,0:T(8,128)(2,1)}, u32[]{:S(2)}) copy-start(bf16[768,384]{1,0:T(8,128)(2,1)} %get-tuple-element.43.right1_ref) | copy-start | bytes 1769476 | tf_op jit(solution)/shard_map/cond
  54.8 31.3 %all-to-all-start.3 = ((bf16[128,56,128]{2,1,0:T(8,128)(2,1)}), bf16[128,56,128]{2,1,0:T(8,128)(2,1)S(1)}, u32[]{:S(2)}, u32[]{:S(2)}) async-start(bf16[128,56,128]{2,1,0:T(8,128)(2,1)} %bitcast.23), calls=%async_computation.3 | async-start | bytes 3670016 | tf_op jit(solution)/shard_map/cond/branch_1_fun/all_to_all | solution.py:630
  58.6 27.5 %copy-start.10 = (s32[128]{0:T(128)S(1)}, s32[128]{0:T(128)}, u32[]{:S(2)}) copy-start(s32[128]{0:T(128)} %get-tuple-element.34.owner_hbm) | copy-start | bytes 1540 | tf_op jit(solution)/shard_map/cond
